TPU v7x, 32 devices: a whole 2x2x4 slice. The times are simulated.
32 devices in a mesh: seq: 4 (over x, core), batch: 8 (over z, y).
Axes of the slice: x: 2, y: 2, z: 4, core: 2. Of those that a mesh axis runs over, the one named last changes fastest.
Arguments:
- values: bfloat16 [24, 512, 768], P('batch', 'seq'), may hold values from -6 to 6
- names: bfloat16 [24, 1536, 768], P('batch', 'seq'), may hold values from -6 to 6
- counts: int32 [24, 512], P('batch', 'seq'), may hold values from 0 to 20, as said below
- valid: int32 [24, 512], P('batch', 'seq'), may hold values from 0 to 1, as said below
- out_grad: bfloat16 [24, 512, 768], P('batch', 'seq'), may hold values from -6 to 6
- master: float32 [9984, 768], P(('seq', 'batch')), may hold values from -2 to 2
- momentum: float32 [9984, 768], P(('seq', 'batch')), may hold values from -0.0048828125 to 0.0048828125
- average: float32 [9984, 768], P(('seq', 'batch')), may hold values from -0.21875 to 0.21875
- vectors: float32 [9216], replicated, may hold values from -1 to 2.1
- vector_momentum: float32 [9216], replicated, may hold values from -0.0048828125 to 0.0048828125
- vector_average: float32 [9216], replicated, may hold values from -3 to 3
Outputs:
- output: bfloat16 [24, 512, 768], P('batch', 'seq')
- grad_values: float32 [24, 512, 768], P('batch', 'seq')
- grad_names: float32 [24, 1536, 768], P('batch', 'seq')
- grad_norm: float32 [], replicated
- new_master: float32 [9984, 768], P(('seq', 'batch'))
- new_momentum: float32 [9984, 768], P(('seq', 'batch'))
- new_average: float32 [9984, 768], P(('seq', 'batch'))
- new_weights: bfloat16 [9984, 768], P(('seq', 'batch'))
- new_vectors: float32 [9216], replicated
- new_vector_momentum: float32 [9216], replicated
- new_vector_average: float32 [9216], replicated
Inputs may be any that keep to these rules, and one draw needn't show every extreme that they name: Positions with valid 0 have count 0. The counts of one row's 128 positions on one device add up to at most 384, and on every device some row reaches it in every draw. Each row is valid on a prefix of 128 positions or more; of the 3 rows of one device, one is valid throughout.
All inputs are finite; a program needn't handle non-finite values.
Results may differ from a plain program's by a relative error of at most 0.018.
The roundings to bfloat16 on the way count: a program that leaves them out, or rounds other values in their place, can miss the bound.
Values may be sent and summed in bfloat16 or wider, within the bound.
A program may use at most 128 MiB of HBM per device.

v0:
```python
import math

import jax
import jax.numpy as jnp
from jax import lax
from jax.sharding import PartitionSpec as P

D = 768
HEAD = 64
FF = 3072
NAME_DEV = 384


norm_eps = 1e-05
step_rate = 40.0
vector_rate = 240.0
momentum_decay = 0.5
average_decay = 0.5
big_negative = -1e30


def layer_norm(value_in, gain, shift):
    centre = jnp.mean(value_in, axis=-1, keepdims=True)
    centred = value_in - centre
    spread = jnp.mean(centred * centred, axis=-1, keepdims=True)
    return centred * lax.rsqrt(spread + norm_eps) * gain + shift


def exact_gelu(value_in):
    return jax.nn.gelu(value_in, approximate=False)


def matmul(first_op, second_op):
    return jnp.dot(first_op, second_op, preferred_element_type=jnp.float32)


def matmul_t(first_op, second_op):
    return lax.dot_general(
        first_op, second_op, (((1,), (1,)), ((), ())), preferred_element_type=jnp.float32
    )


def tokens_t(first_op, second_op):
    return lax.dot_general(
        first_op, second_op, (((0,), (0,)), ((), ())), preferred_element_type=jnp.float32
    )


def split_heads(array_in):
    return array_in.reshape(array_in.shape[0], array_in.shape[1], array_in.shape[2] // HEAD, HEAD)


def block_scores(query_part, key_part, mask_part):
    scores = jnp.einsum(
        "bqhd,bkhd->bhqk",
        split_heads(query_part),
        split_heads(key_part),
        preferred_element_type=jnp.float32,
    ) * HEAD ** (-0.5)
    return jnp.where(mask_part[:, None, None, :] > 0, scores, big_negative)


def attend_block(pieces):
    query_part, key_part, value_part, mask_part = pieces
    scores = block_scores(query_part, key_part, mask_part)
    top_score = jnp.max(scores, axis=-1, keepdims=True)
    exp_scores = jnp.exp(scores - top_score)
    exp_total = jnp.sum(exp_scores, axis=-1, keepdims=True)
    prob = (exp_scores / exp_total).astype(jnp.bfloat16)
    context = jnp.einsum(
        "bhqk,bkhd->bqhd", prob, split_heads(value_part), preferred_element_type=jnp.float32
    )
    log_total = (top_score + jnp.log(exp_total))[..., 0]
    return (context.reshape(query_part.shape).astype(jnp.bfloat16), log_total)


def attend_back(pieces):
    query_part, key_part, value_part, mask_part, log_total, grad_context = pieces
    scores = block_scores(query_part, key_part, mask_part)
    prob = jnp.exp(scores - log_total[..., None])
    grad_heads = split_heads(grad_context)
    grad_prob = jnp.einsum(
        "bqhd,bkhd->bhqk", grad_heads, split_heads(value_part), preferred_element_type=jnp.float32
    )
    grad_value = jnp.einsum(
        "bhqk,bqhd->bkhd", prob.astype(jnp.bfloat16), grad_heads, preferred_element_type=jnp.float32
    )
    inner = jnp.sum(grad_prob * prob, axis=-1, keepdims=True)
    grad_scores = (prob * (grad_prob - inner)).astype(jnp.bfloat16)
    scale = HEAD ** (-0.5)
    grad_query = (
        jnp.einsum(
            "bhqk,bkhd->bqhd",
            grad_scores,
            split_heads(key_part),
            preferred_element_type=jnp.float32,
        )
        * scale
    )
    grad_key = (
        jnp.einsum(
            "bhqk,bqhd->bkhd",
            grad_scores,
            split_heads(query_part),
            preferred_element_type=jnp.float32,
        )
        * scale
    )
    return (
        grad_query.reshape(query_part.shape),
        grad_key.reshape(key_part.shape),
        grad_value.reshape(value_part.shape),
    )


def apply_update(weight, moment, mean_state, gradient, clip_factor, rate):
    clipped = gradient * clip_factor
    new_moment = momentum_decay * moment + clipped
    new_weight = weight - rate * (clipped + momentum_decay * new_moment)
    new_mean = average_decay * mean_state + (1.0 - average_decay) * new_weight
    return (new_weight, new_moment, new_mean)


def local(
    values,
    names,
    counts,
    valid,
    out_grad,
    master,
    momentum,
    average,
    vectors,
    vector_momentum,
    vector_average,
):
    row_count, row_span, width = values.shape
    token_count = row_count * row_span
    weights = lax.all_gather(master.astype(jnp.bfloat16), ("seq", "batch"), axis=0, tiled=True)
    w_qkv = weights[0 : 3 * D]
    w_attn = weights[3 * D : 4 * D]
    w_unite = weights[4 * D : 5 * D]
    w_in = weights[5 * D : 5 * D + FF]
    w_down = weights[5 * D + FF : 5 * D + 2 * FF]
    bias_q = vectors[0:D]
    bias_v = vectors[D : 2 * D]
    bias_o = vectors[2 * D : 3 * D]
    gain_one = vectors[3 * D : 4 * D]
    shift_one = vectors[4 * D : 5 * D]
    bias_down = vectors[5 * D : 6 * D]
    gain_two = vectors[6 * D : 7 * D]
    shift_two = vectors[7 * D : 8 * D]
    bias_in = vectors[8 * D : 8 * D + FF]
    slot_ends = jnp.cumsum(counts, axis=1)
    slot_starts = slot_ends - counts
    slot_ids = jnp.arange(NAME_DEV, dtype=jnp.int32)
    inside = (slot_ids >= slot_starts[:, :, None]) & (slot_ids < slot_ends[:, :, None])
    summed = jnp.einsum(
        "rtn,rnd->rtd", inside.astype(jnp.bfloat16), names, preferred_element_type=jnp.float32
    )
    divisor = jnp.maximum(counts.astype(jnp.float32), 1.0)[:, :, None]
    pooled = (summed / divisor).astype(jnp.bfloat16).reshape(token_count, D)
    united = values.reshape(token_count, D).astype(jnp.float32) + matmul(pooled, w_unite)
    first = united.astype(jnp.bfloat16)
    projected = matmul_t(first, w_qkv)
    query = (projected[:, 0:D] + bias_q).astype(jnp.bfloat16).reshape(row_count, row_span, D)
    key_proj = projected[:, D : 2 * D].astype(jnp.bfloat16).reshape(row_count, row_span, D)
    value_proj = (
        (projected[:, 2 * D : 3 * D] + bias_v).astype(jnp.bfloat16).reshape(row_count, row_span, D)
    )
    key_all, value_all, mask_all = (
        lax.all_gather(key_proj, "seq", axis=1, tiled=True),
        lax.all_gather(value_proj, "seq", axis=1, tiled=True),
        lax.all_gather(valid.astype(jnp.bfloat16), "seq", axis=1, tiled=True),
    )
    block_rows = math.gcd(row_count, max(1, 512 // row_span))
    block_count = row_count // block_rows

    def blocked(array_in):
        return array_in.reshape((block_count, block_rows) + array_in.shape[1:])

    context, log_total = lax.map(
        attend_block, (blocked(query), blocked(key_all), blocked(value_all), blocked(mask_all))
    )
    context = context.reshape(token_count, D)
    attn_out = matmul(context, w_attn) + bias_o
    normed, norm_one_back = jax.vjp(layer_norm, united + attn_out, gain_one, shift_one)
    lowered = normed.astype(jnp.bfloat16)
    up_proj = matmul_t(lowered, w_in) + bias_in
    activated, gelu_back = jax.vjp(exact_gelu, up_proj)
    hidden = activated.astype(jnp.bfloat16)
    down_proj = matmul(hidden, w_down) + bias_down
    result, norm_two_back = jax.vjp(layer_norm, normed + down_proj, gain_two, shift_two)
    output = result.astype(jnp.bfloat16).reshape(row_count, row_span, D)
    grad_two, grad_gain_two, grad_shift_two = norm_two_back(
        out_grad.reshape(token_count, D).astype(jnp.float32)
    )
    grad_down = grad_two.astype(jnp.bfloat16)
    grad_bias_down = jnp.sum(grad_down.astype(jnp.float32), axis=0)
    grad_w_down = tokens_t(hidden, grad_down)
    grad_hidden = matmul_t(grad_down, w_down)
    grad_up = gelu_back(grad_hidden)[0].astype(jnp.bfloat16)
    grad_bias_in = jnp.sum(grad_up.astype(jnp.float32), axis=0)
    grad_w_in = tokens_t(grad_up, lowered)
    grad_one, grad_gain_one, grad_shift_one = norm_one_back(grad_two + matmul(grad_up, w_in))
    grad_attn = grad_one.astype(jnp.bfloat16)
    grad_bias_o = jnp.sum(grad_attn.astype(jnp.float32), axis=0)
    grad_w_attn = tokens_t(context, grad_attn)
    grad_context = matmul_t(grad_attn, w_attn).astype(jnp.bfloat16).reshape(row_count, row_span, D)
    grad_query, key_terms, value_terms = lax.map(
        attend_back,
        (
            blocked(query),
            blocked(key_all),
            blocked(value_all),
            blocked(mask_all),
            log_total,
            blocked(grad_context),
        ),
    )
    grad_key, grad_value = (
        lax.psum_scatter(
            key_terms.reshape(row_count, -1, D).astype(jnp.bfloat16),
            "seq",
            scatter_dimension=1,
            tiled=True,
        ).astype(jnp.float32),
        lax.psum_scatter(
            value_terms.reshape(row_count, -1, D).astype(jnp.bfloat16),
            "seq",
            scatter_dimension=1,
            tiled=True,
        ).astype(jnp.float32),
    )
    grad_q = grad_query.reshape(token_count, D).astype(jnp.bfloat16)
    grad_k = grad_key.reshape(token_count, D).astype(jnp.bfloat16)
    grad_v = grad_value.reshape(token_count, D).astype(jnp.bfloat16)
    grad_bias_q = jnp.sum(grad_q.astype(jnp.float32), axis=0)
    grad_bias_v = jnp.sum(grad_v.astype(jnp.float32), axis=0)
    grad_qkv = jnp.concatenate([grad_q, grad_k, grad_v], axis=1)
    grad_w_qkv = tokens_t(grad_qkv, first)
    grad_united = grad_one + matmul(grad_qkv, w_qkv)
    grad_unite = grad_united.astype(jnp.bfloat16)
    grad_w_unite = tokens_t(pooled, grad_unite)
    grad_pooled = lax.optimization_barrier(
        matmul_t(grad_unite, w_unite).astype(jnp.bfloat16)
    ).astype(jnp.float32)
    grad_pooled = grad_pooled.reshape(row_count, row_span, D) / divisor
    grad_names = jnp.einsum(
        "rtn,rtd->rnd", inside.astype(jnp.float32), grad_pooled, precision=lax.Precision.HIGHEST
    )
    grad_values = grad_united.reshape(row_count, row_span, D)
    vector_grads = jnp.concatenate(
        [
            grad_bias_q,
            grad_bias_v,
            grad_bias_o,
            grad_gain_one,
            grad_shift_one,
            grad_bias_down,
            grad_gain_two,
            grad_shift_two,
            grad_bias_in,
        ]
    )
    grads = jnp.concatenate([grad_w_qkv, grad_w_attn, grad_w_unite, grad_w_in, grad_w_down], axis=0)
    owned = lax.psum_scatter(grads, ("seq", "batch"), scatter_dimension=0, tiled=True)
    local_squares = jnp.sum(owned * owned)
    vector_total, matrix_squares = lax.psum((vector_grads, local_squares), ("seq", "batch"))
    grad_norm = jnp.sqrt(matrix_squares + jnp.sum(vector_total * vector_total))
    clip_factor = 1.0 / jnp.maximum(grad_norm, 1.0)
    new_master, new_momentum, new_average = apply_update(
        master, momentum, average, owned, clip_factor, step_rate
    )
    new_vectors, new_vector_momentum, new_vector_average = apply_update(
        vectors, vector_momentum, vector_average, vector_total, clip_factor, vector_rate
    )
    return (
        output,
        grad_values,
        grad_names,
        grad_norm,
        new_master,
        new_momentum,
        new_average,
        new_master.astype(jnp.bfloat16),
        new_vectors,
        new_vector_momentum,
        new_vector_average,
    )


def solution(mesh):
    return jax.shard_map(
        local,
        mesh=mesh,
        in_specs=(
            P("batch", "seq", None),
            P("batch", "seq", None),
            P("batch", "seq"),
            P("batch", "seq"),
            P("batch", "seq", None),
            P(("seq", "batch"), None),
            P(("seq", "batch"), None),
            P(("seq", "batch"), None),
            P(),
            P(),
            P(),
        ),
        out_specs=(
            P("batch", "seq", None),
            P("batch", "seq", None),
            P("batch", "seq", None),
            P(),
            P(("seq", "batch"), None),
            P(("seq", "batch"), None),
            P(("seq", "batch"), None),
            P(("seq", "batch"), None),
            P(),
            P(),
            P(),
        ),
        check_vma=False,
    )
```

profile of v0, /device:TPU:0, one launch (start us, length us, event | category | flops | bytes accessed | tf_op | source)
XLA Modules:
  0.0 728.5 jit_solution(3177972717825030798)
XLA Ops:
  7.2 2.1 convert_element_type.154
  13.0 109.6 %all-gather.4.cloned.1.call-done = bf16[9984,768]{1,0:T(8,128)(2,1)} async-done(((bf16[312,768]{1,0:T(8,128)(2,1)}), bf16[9984,768]{1,0:T(8,128)(2,1)}) %all-gather.4.cloned.1.call-update) | async-done | bytes 15335440 | tf_op jit(solution)/shard_map/all_gather | solution.py:139
  122.6 1.9 convolution_add_fusion.2
  124.5 5.8 fusion.23
  130.3 1.3 slice.114
  132.8 1.8 fusion.41
  135.8 5.1 all_gather.14
  142.0 13.4 %all-gather.8.cloned.1.call-done = bf16[3,512,768]{1,2,0:T(8,128)(2,1)} async-done(((bf16[3,128,768]{1,2,0:T(8,128)(2,1)}), bf16[3,512,768]{1,2,0:T(8,128)(2,1)}) %all-gather.8.cloned.1.call-update) | async-done | bytes 2359312 | tf_op jit(solution)/shard_map/all_gather | solution.py:172
  155.4 26.5 %all-gather.6.cloned.1.call-done = bf16[3,512,768]{1,2,0:T(8,128)(2,1)} async-done(((bf16[3,128,768]{1,2,0:T(8,128)(2,1)}), bf16[3,512,768]{1,2,0:T(8,128)(2,1)}) %all-gather.6.cloned.1.call-update) | async-done | bytes 2359312 | tf_op jit(solution)/shard_map/all_gather | solution.py:173
  181.9 18.5 %while.26 = (s32[]{:T(128)}, bf16[3,1,128,768]{3,2,0,1:T(8,128)(2,1)S(1)}, f32[3,1,12,128]{3,2,1,0:T(8,128)}, bf16[3,1,512,768]{2,3,1,0:T(8,128)(2,1)}, bf16[3,1...) while((s32[]{:T(128)}, ...), condition=%wide.region_4.5_spmd, body=%wide.region_1.4_spmd.sunk | while | flops 210861056 | bytes 15783025 | solution.py:182
  182.9 1.5 constant_dynamic-slice_fusion.14
  186.0 1.3 fusion.125
  189.1 1.5 constant_dynamic-slice_fusion.14
  192.1 1.3 fusion.125
  195.2 1.5 constant_dynamic-slice_fusion.14
  198.3 1.3 fusion.125
  200.5 2.2 fusion.76
  203.0 15.3 %multiply_convert_fusion.1 = (bf16[384,3072]{1,0:T(8,128)(2,1)S(1)}, f32[384,3072]{1,0:T(8,128)}, f32[384,3072]{1,0:T(8,128)}) fusion(f32[3072]{0:T(1024)S(1)} %slice-done.4, bf16[9984,768]{1,0:T(8,128)(2,1)} %all-gather.4.cloned.1.call-done, f32[384,768]{1,0:T(8,128)S(1)} %get-tuple-element.219, f32[768]{0:T(1024)S(1)} %get-tuple-element.212, ...), kind=kOutput, calls=%fused_computation.39 | convolution fusion | flops 1891270656 | bytes 17716224 | tf_op jit(solution)/shard_map/dot_general | solution.py:38
  218.4 2.1 fusion.77
  222.0 1.4 fusion.73
  224.1 6.9 convert_reduce_fusion
  231.0 2.8 multiply_reduce_fusion.1
  236.9 1.5 convolution_convert_fusion.1
  238.5 54.6 %while.27 = (s32[]{:T(128)}, bf16[3,1,128,768]{3,2,0,1:T(8,128)(2,1)}, bf16[3,1,512,768]{3,2,0,1:T(8,128)(2,1)}, bf16[3,1,512,768]{3,2,0,1:T(8,128)(2,1)}, bf16[...) while((s32[]{:T(128)}, ...), condition=%wide.region_15.16_spmd, body=%wide.region_13.15_spmd.sunk | while | flops 511376384 | bytes 49383684 | solution.py:210
  241.8 2.1 constant_dynamic-slice_fusion.19
  248.0 2.3 copy.77
  250.3 1.8 multiply_reduce_fusion.8
  260.0 2.1 constant_dynamic-slice_fusion.19
  266.2 2.3 copy.77
  268.5 1.8 multiply_reduce_fusion.8
  278.2 2.1 constant_dynamic-slice_fusion.19
  284.4 2.3 copy.77
  286.7 1.8 multiply_reduce_fusion.8
  293.7 32.6 %reduce-scatter.4.cloned.1.call-done = bf16[3,128,768]{2,1,0:T(8,128)(2,1)} async-done(((bf16[3,512,768]{2,1,0:T(8,128)(2,1)}), bf16[3,128,768]{2,1,0:T(8,128)(2,1)}) %reduce-scatter.4.cloned.1.call-update) | async-done | bytes 589840 | tf_op jit(solution)/shard_map/reduce_scatter | solution.py:222
  326.3 35.6 %reduce-scatter.6.cloned.1.call-done = bf16[3,128,768]{2,1,0:T(8,128)(2,1)} async-done(((bf16[3,512,768]{2,1,0:T(8,128)(2,1)}), bf16[3,128,768]{2,1,0:T(8,128)(2,1)}) %reduce-scatter.6.cloned.1.call-update) | async-done | bytes 589840 | tf_op jit(solution)/shard_map/reduce_scatter | solution.py:228
  361.9 6.3 convolution_dynamic-update-slice_fusion
  368.2 2.3 convolution_dynamic-update-slice_fusion.4
  370.5 3.6 fusion.34
  374.2 2.2 convolution_dynamic-update-slice_fusion.3
  377.5 5.6 convolution_dynamic-update-slice_fusion.2
  383.1 5.1 convolution_dynamic-update-slice_fusion.1
  389.5 1.9 convolution_convert_fusion
  391.8 274.3 %reduce-scatter.8.cloned.1.call-done = f32[312,768]{1,0:T(8,128)} async-done(((f32[9984,768]{1,0:T(8,128)}), f32[312,768]{1,0:T(8,128)}) %reduce-scatter.8.cloned.1.call-update) | async-done | bytes 958480 | tf_op jit(solution)/shard_map/reduce_scatter | solution.py:267
  666.1 2.0 multiply_reduce_fusion.5
  668.2 3.5 fusion.43
  671.7 40.7 %all-reduce = (f32[]{:T(128)}, f32[9216]{0:T(1024)S(1)}) all-reduce(f32[]{:T(128)} %multiply_reduce_fusion.5, f32[9216]{0:T(1024)S(1)} %constant_dynamic-update-slice_fusion.8), channel_id=1, replica_groups=mesh['seq'=4,'batch'=8] {'seq','batch'}, use_global_device_ids=true, to_apply=%region_20.21 | all-reduce | flops 9217 | bytes 73736 | tf_op jit(solution)/shard_map/psum | solution.py:269
  715.1 2.8 fusion.71
  717.9 2.6 add_multiply_fusion
  (269 shorter events, 62.7 us)
Async XLA Ops:
  7.2 5.3 copy-start
  7.2 115.4 %all-gather.4.cloned.1.call-start = ((), (), s32[]{:S(2)}) async-start(), calls=%async_computation.3 | async-start | bytes 15814656 | tf_op jit(solution)/shard_map/all_gather | solution.py:139
  9.4 113.2 %copy-start.28 = (bf16[3,128,768]{2,1,0:T(8,128)(2,1)S(1)}, bf16[3,128,768]{2,1,0:T(8,128)(2,1)}, u32[]{:S(2)}) copy-start(bf16[3,128,768]{2,1,0:T(8,128)(2,1)} %param.15) | copy-start | bytes 1769476
  9.4 146.0 %all-gather.8.cloned.1.call-start = ((), (), s32[]{:S(2)}) async-start(), calls=%async_computation.5 | async-start | bytes 2949120 | tf_op jit(solution)/shard_map/all_gather | solution.py:172
  10.5 112.1 %copy-start.48 = (s32[3,128]{1,0:T(4,128)}, s32[3,128]{1,0:T(4,128)S(1)}, u32[]{:S(2)}) copy-start(s32[3,128]{1,0:T(4,128)S(1)} %reduce_window_sum.11) | copy-start | bytes 4612
  13.0 117.3 %copy-start.24 = (bf16[3,128,768]{2,1,0:T(8,128)(2,1)}, bf16[3,128,768]{2,1,0:T(8,128)(2,1)S(1)}, u32[]{:S(2)}) copy-start(bf16[3,128,768]{2,1,0:T(8,128)(2,1)S(1)} %fusion.40) | copy-start | bytes 1769476
  124.5 76.0 %copy-start.9 = (f32[384,768]{1,0:T(8,128)}, f32[384,768]{1,0:T(8,128)S(1)}, u32[]{:S(2)}) copy-start(f32[384,768]{1,0:T(8,128)S(1)} %convolution_add_fusion.2) | copy-start | bytes 3538948
  124.5 8.3 %copy-start.31 = (f32[9216]{0:T(1024)S(1)}, f32[9216]{0:T(1024)}, u32[]{:S(2)}) copy-start(f32[9216]{0:T(1024)} %param.23) | copy-start | bytes 110596
  132.7 49.2 %all-gather.6.cloned.1.call-start = ((), (), s32[]{:S(2)}) async-start(), calls=%async_computation.4 | async-start | bytes 2949120 | tf_op jit(solution)/shard_map/all_gather | solution.py:173
  132.8 85.6 %copy-start.44 = (f32[768]{0:T(1024)}, f32[768]{0:T(1024)S(1)}, u32[]{:S(2)}) copy-start(f32[768]{0:T(1024)S(1)} %get-tuple-element.212) | copy-start | bytes 9220
  132.8 101.0 %copy-start.35 = (f32[768]{0:T(1024)}, f32[768]{0:T(1024)S(1)}, u32[]{:S(2)}) copy-start(f32[768]{0:T(1024)S(1)} %get-tuple-element.213) | copy-start | bytes 9220
  135.7 190.6 %reduce-scatter.4.cloned.1.call-start = ((), (), s32[]{:S(2)}) async-start(), calls=%async_computation.6 | async-start | bytes 2949120 | tf_op jit(solution)/shard_map/reduce_scatter | solution.py:222
  200.4 17.9 %copy-start.20 = (bf16[3,1,128,768]{3,2,0,1:T(8,128)(2,1)}, bf16[3,1,128,768]{3,2,0,1:T(8,128)(2,1)S(1)}, u32[]{:S(2)}) copy-start(bf16[3,1,128,768]{3,2,0,1:T(8,128)(2,1)S(1)} %get-tuple-element.103) | copy-start | bytes 1769476
  200.5 17.9 %slice-start = ((s8[15335424]{0:T(1024)(128)(4,1)}), s8[4194304]{0:T(1024)(128)(4,1)S(1)}, s32[]{:S(2)}) async-start(s8[15335424]{0:T(1024)(128)(4,1)} %bitcast.168), calls=%async_computation.9 | async-start | bytes 8388608
  202.7 31.2 %copy-start.5 = (f32[384,768]{1,0:T(8,128)}, f32[384,768]{1,0:T(8,128)S(1)}, u32[]{:S(2)}) copy-start(f32[384,768]{1,0:T(8,128)S(1)} %get-tuple-element.219) | copy-start | bytes 3538948
  202.7 31.2 %copy-start.37 = (f32[384]{0:T(512)}, f32[384]{0:T(512)S(1)}, u32[]{:S(2)}) copy-start(f32[384]{0:T(512)S(1)} %broadcast_multiply_fusion.1) | copy-start | bytes 4612
  203.0 30.9 %copy-start.39 = (f32[384]{0:T(512)}, f32[384]{0:T(512)S(1)}, u32[]{:S(2)}) copy-start(f32[384]{0:T(512)S(1)} %fusion.65) | copy-start | bytes 4612
  203.0 15.4 %slice-start.1 = ((s8[15335424]{0:T(1024)(128)(4,1)}), s8[4194304]{0:T(1024)(128)(4,1)S(1)}, s32[]{:S(2)}) async-start(s8[15335424]{0:T(1024)(128)(4,1)} %bitcast.168), calls=%async_computation.10 | async-start | bytes 8388608
  203.0 15.4 %slice-start.2 = ((s8[15335424]{0:T(1024)(128)(4,1)}), s8[4194304]{0:T(1024)(128)(4,1)S(1)}, s32[]{:S(2)}) async-start(s8[15335424]{0:T(1024)(128)(4,1)} %bitcast.168), calls=%async_computation.11 | async-start | bytes 8388608
  203.0 15.4 %slice-start.3 = ((s8[15335424]{0:T(1024)(128)(4,1)}), s8[2752512]{0:T(1024)(128)(4,1)S(1)}, s32[]{:S(2)}) async-start(s8[15335424]{0:T(1024)(128)(4,1)} %bitcast.168), calls=%async_computation.12 | async-start | bytes 5505024
  224.1 6.9 copy-start.22
  234.4 4.1 copy-start.50
  240.8 5.1 copy-start.46
  259.0 5.1 copy-start.46
  277.2 5.1 copy-start.46
  293.1 68.9 %copy-start.10 = (f32[384,768]{1,0:T(8,128)S(1)}, f32[384,768]{1,0:T(8,128)}, u32[]{:S(2)}) copy-start(f32[384,768]{1,0:T(8,128)} %copy-done.9) | copy-start | bytes 3538948
  293.1 68.9 %copy-start.29 = (bf16[3,1,128,768]{3,2,0,1:T(8,128)(2,1)S(1)}, bf16[3,1,128,768]{3,2,0,1:T(8,128)(2,1)}, u32[]{:S(2)}) copy-start(bf16[3,1,128,768]{3,2,0,1:T(8,128)(2,1)} %get-tuple-element.105) | copy-start | bytes 1769476
  293.1 68.8 %reduce-scatter.6.cloned.1.call-start = ((), (), s32[]{:S(2)}) async-start(), calls=%async_computation.7 | async-start | bytes 2949120 | tf_op jit(solution)/shard_map/reduce_scatter | solution.py:228
  293.7 372.5 %reduce-scatter.8.cloned.1.call-start = ((), (), s32[]{:S(2)}) async-start(), calls=%async_computation.8 | async-start | bytes 31629312 | tf_op jit(solution)/shard_map/reduce_scatter | solution.py:267
  361.9 6.3 copy-start.21
  361.9 6.3 copy-start.27
  370.5 3.6 copy-start.25
  374.2 15.4 %copy-start.13 = (f32[384,768]{1,0:T(8,128)}, f32[384,768]{1,0:T(8,128)S(1)}, u32[]{:S(2)}) copy-start(f32[384,768]{1,0:T(8,128)S(1)} %fusion.34) | copy-start | bytes 3538948
  377.5 5.6 copy-start.19
  377.5 5.6 copy-start.23
  388.3 3.4 copy-start.53
  388.3 3.4 copy-start.52
  388.3 3.4 copy-start.42
  388.3 3.5 copy-start.41
  388.3 3.5 copy-start.47
  388.3 279.9 %copy-start.49 = (s32[3,128]{1,0:T(4,128)S(1)}, s32[3,128]{1,0:T(4,128)}, u32[]{:S(2)}) copy-start(s32[3,128]{1,0:T(4,128)} %copy-done.48) | copy-start | bytes 4612
  388.3 279.9 %copy-start.55 = (s32[3,128]{1,0:T(4,128)S(1)}, s32[3,128]{1,0:T(4,128)}, u32[]{:S(2)}) copy-start(s32[3,128]{1,0:T(4,128)} %copy-done.54) | copy-start | bytes 4612
  388.3 279.9 %copy-start.58 = (f32[3,128]{1,0:T(4,128)S(1)}, f32[3,128]{1,0:T(4,128)}, u32[]{:S(2)}) copy-start(f32[3,128]{1,0:T(4,128)} %copy-done.57) | copy-start | bytes 4612
  391.5 323.0 %copy-start.32 = (f32[9216]{0:T(1024)S(1)}, f32[9216]{0:T(1024)}, u32[]{:S(2)}) copy-start(f32[9216]{0:T(1024)} %param.23) | copy-start | bytes 110596
  391.5 323.0 %copy-start.33 = (f32[9216]{0:T(1024)S(1)}, f32[9216]{0:T(1024)}, u32[]{:S(2)}) copy-start(f32[9216]{0:T(1024)} %param.25) | copy-start | bytes 110596
  391.5 323.0 %copy-start.34 = (f32[9216]{0:T(1024)S(1)}, f32[9216]{0:T(1024)}, u32[]{:S(2)}) copy-start(f32[9216]{0:T(1024)} %param.24) | copy-start | bytes 110596
  391.6 323.5 %copy-start.15 = (f32[312,768]{1,0:T(8,128)S(1)}, f32[312,768]{1,0:T(8,128)}, u32[]{:S(2)}) copy-start(f32[312,768]{1,0:T(8,128)} %param.20) | copy-start | bytes 2875396
  714.5 6.1 copy-start.1
  (31 other events, 63.8 us)
Sparse Core Ops, SparseCore 0:
  11.5 110.9 all-gather.3
  132.8 22.5 all-gather.7
  157.5 24.3 all-gather.5
  293.2 33.0 reduce-scatter.3
  328.8 33.0 reduce-scatter.5
  388.4 277.7 reduce-scatter.7
where the time goes:
time: 730 us; the launch traced here: 729 us
  waiting for transfers between devices  493 us (68%)
  matrix products  90.5 us (12%)
  local copies, waits for them, and re-layouts  53.3 us (7%)
  blocking collectives  45.8 us (6%)
  other arithmetic  28.3 us (4%)
  between operations  17.4 us (2%)
    reduce_scatter x1, waiting for transfers between devices, local(): lax.psum_scatter(grads, ('seq', 'batch'), scatter_dimension=0, tiled=True)  274 us
    all_gather x1, waiting for transfers between devices, local(): lax.all_gather(master.astype(jnp.bfloat16), ('seq', 'batch'), axis=0, til...  110 us
    psum x1, blocking collectives, local(): lax.psum((vector_grads, local_squares), ('seq', 'batch'))  40.7 us
    reduce_scatter x1, waiting for transfers between devices, local(): lax.psum_scatter(value_terms.reshape(row_count, -1, D).astype(jnp.bfloat1...  35.6 us
    reduce_scatter x1, waiting for transfers between devices, local(): lax.psum_scatter(key_terms.reshape(row_count, -1, D).astype(jnp.bfloat16)...  32.6 us
    dot_general x5, matrix products, matmul_t(): lax.dot_general(first_op, second_op, (((1,), (1,)), ((), ())), preferred_...  31.5 us
    all_gather x1, waiting for transfers between devices, local(): lax.all_gather(value_proj, 'seq', axis=1, tiled=True)  26.5 us
    dynamic_slice x21, local copies, waits for them, and re-layouts, local(): lax.map(attend_block, (blocked(query), blocked(key_all), blocked(value_al...  23.2 us
  transfers between devices with their start and end apart: 6, of which 6 were waited for; matrix products, arithmetic and copies ran while one was open for 1% of the time, Pallas kernels for 0%

commit v1 on v0

--- a/solution.py
+++ b/solution.py
@@ -1,9 +1,14 @@
+import functools
 import math
 
 import jax
 import jax.numpy as jnp
 from jax import lax
+from jax.experimental import pallas as pl
+from jax.experimental.pallas import tpu as pltpu
 from jax.sharding import PartitionSpec as P
+
+MESH = pl.DeviceIdType.MESH
 
 D = 768
 HEAD = 64
@@ -121,7 +126,139 @@
     return (new_weight, new_moment, new_mean)
 
 
+def place():
+    s=lax.axis_index("seq"); b=lax.axis_index("batch")
+    return s//2, s%2, b//2, b%2
+def when(cond,fn):
+    if cond is None or cond is True: fn()
+    elif cond is False: pass
+    else: pl.when(cond)(fn)
+
+class Gather:
+    cols=((0,512),(512,256))
+    def __init__(self,w,stage,send_sem,recv_sem,sib_sem):
+        self.w=w; self.stage=stage; self.ss=send_sem; self.rs=recv_sem; self.bs=sib_sem
+        self.x,self.c,self.z,self.y=place()
+        self.sent=[]
+    def dev(self,d):
+        x,c,z,y=self.x,self.c,self.z,self.y
+        return {"x":{"seq":(1-x)*2+c,"batch":z*2+y},"y":{"seq":x*2+c,"batch":z*2+1-y},"c":{"seq":x*2+1-c,"batch":z*2+y},
+                "u":{"seq":x*2+c,"batch":jnp.minimum(z+1,3)*2+y},"d":{"seq":x*2+c,"batch":jnp.maximum(z-1,0)*2+y}}[d]
+    def region(self,t,x0,z0,y0,n,c=None):
+        c=self.c if c is None else c
+        off=pl.multiple_of((2*x0+c)*2496+z0*624+320*y0,16)
+        c0,cn=self.cols[t]
+        return self.w.at[pl.ds(off,n),pl.ds(c0,cn)]
+    def both(self,y0,cond,fn):
+        if isinstance(y0,int):
+            when(cond,lambda: fn(320 if y0==0 else 304))
+        else:
+            c0=(y0==0); c1=(y0==1)
+            if cond is not None: c0=jnp.logical_and(c0,cond); c1=jnp.logical_and(c1,cond)
+            pl.when(c0)(lambda: fn(320)); pl.when(c1)(lambda: fn(304))
+    def copy(self,t,x0,z0,y0,d,n,own):
+        c0,cn=self.cols[t]
+        dst=self.region(t,x0,z0,y0,n)
+        src=self.stage.at[pl.ds(0,n),pl.ds(c0,cn)] if own else dst
+        k=x0*8+z0*2+y0
+        i={"u":0,"d":1,"x":2,"y":2,"c":3}[d]
+        if d in "xy" and ((t==0)!=(d=="y")): i=4
+        rsem=self.bs.at[t,k] if d=="c" else self.rs.at[t,k]
+        return pltpu.make_async_remote_copy(src_ref=src,dst_ref=dst,send_sem=self.ss.at[t,k,i],recv_sem=rsem,device_id=self.dev(d),device_id_type=MESH)
+    def send(self,t,x0,z0,y0,dirs,own=False,cond=None):
+        for d,dc in dirs:
+            cc=cond if dc is None else (dc if cond is None else jnp.logical_and(cond,dc))
+            self.both(y0,cc,lambda n,d=d: self.copy(t,x0,z0,y0,d,n,own).start())
+            self.sent.append((t,x0,z0,y0,d,own,cc))
+    def recv(self,t,x0,z0,y0,cond=None):
+        self.both(y0,cond,lambda n: self.copy(t,x0,z0,y0,"x",n,False).wait_recv())
+    def recv_sib(self,t,x0,z0,y0):
+        def f(n):
+            r=self.region(t,x0,z0,y0,n,c=1-self.c)
+            k=x0*8+z0*2+y0
+            pltpu.make_async_remote_copy(src_ref=r,dst_ref=r,send_sem=self.ss.at[t,k,0],recv_sem=self.bs.at[t,k],device_id=self.dev("c"),device_id_type=MESH).wait_recv()
+        self.both(y0,None,f)
+    def events(self):
+        x,c,z,y=self.x,self.c,self.z,self.y
+        up=z<3; dn=z>0
+        ev=[]
+        def start():
+            self.send(0,x,z,y,[("x",None),("u",up),("d",dn),("y",None),("c",None)],own=True)
+            self.send(1,x,z,y,[("y",None),("u",up),("d",dn),("x",None),("c",None)],own=True)
+        ev.append(start)
+        def first():
+            self.recv(0,1-x,z,y); self.send(0,1-x,z,y,[("u",up),("d",dn),("y",None),("c",None)])
+            self.recv(1,x,z,1-y); self.send(1,x,z,1-y,[("u",up),("d",dn),("x",None),("c",None)])
+        ev.append(first)
+        for d in (1,2,3):
+            for j in (0,1):
+                def zstep(d=d,j=j):
+                    for t in (0,1):
+                        for sgn in (-1,1):
+                            z0=z+sgn*d
+                            ok=(z0>=0) if sgn<0 else (z0<=3)
+                            x0,y0=(x if j==0 else 1-x, y) if t==0 else (x, y if j==0 else 1-y)
+                            self.recv(t,x0,z0,y0,cond=ok)
+                            relay=[("u",up)] if sgn<0 else [("d",dn)]
+                            self.send(t,x0,z0,y0,relay+[("y" if t==0 else "x",None),("c",None)],cond=ok)
+                ev.append(zstep)
+        for z0 in range(4):
+            for j in (0,1):
+                def leaf(z0=z0,j=j):
+                    self.recv(0,j,z0,1-y); self.send(0,j,z0,1-y,[("c",None)])
+                    self.recv(1,1-x,z0,j); self.send(1,1-x,z0,j,[("c",None)])
+                ev.append(leaf)
+        return ev
+    def finish(self):
+        for t in (0,1):
+            for x0 in (0,1):
+                for z0 in range(4):
+                    for y0 in (0,1):
+                        self.recv_sib(t,x0,z0,y0)
+        for t,x0,z0,y0,d,own,cc in self.sent:
+            self.both(y0,cc,lambda n: self.copy(t,x0,z0,y0,d,n,own).wait_send())
+
+def barrier(g):
+    bar=pltpu.get_barrier_semaphore()
+    x,c,z,y=g.x,g.c,g.z,g.y
+    for d,cond in (("x",None),("y",None),("c",None),("u",z<3),("d",z>0)):
+        when(cond,lambda d=d: pl.semaphore_signal(bar,1,device_id=g.dev(d),device_id_type=MESH))
+    pl.semaphore_wait(bar,3+(z<3).astype(jnp.int32)+(z>0).astype(jnp.int32))
+
+def ag_kernel(master,w,stage,edge,edge_sem,send_sem,recv_sem,sib_sem,own_sem):
+    g=Gather(w,stage,send_sem,recv_sem,sib_sem)
+    x,c,z,y=g.x,g.c,g.z,g.y
+    barrier(g)
+    ecopy=pltpu.make_async_remote_copy(src_ref=master.at[pl.ds(0,8)],dst_ref=edge,send_sem=edge_sem.at[0],recv_sem=edge_sem.at[1],device_id=g.dev("y"),device_id_type=MESH)
+    @pl.when(y==1)
+    def _():
+        ecopy.start()
+        stage[0:304]=master[8:312].astype(jnp.bfloat16)
+        stage[304:320]=jnp.zeros((16,768),jnp.bfloat16)
+    @pl.when(y==0)
+    def _():
+        stage[0:304]=master[0:304].astype(jnp.bfloat16)
+        ecopy.wait_recv()
+        stage[304:320]=jnp.concatenate([master[304:312],edge[...]],axis=0).astype(jnp.bfloat16)
+    def own(n):
+        off=pl.multiple_of((2*x+c)*2496+z*624+320*y,16)
+        return pltpu.make_async_copy(stage.at[pl.ds(0,n)],w.at[pl.ds(off,n)],own_sem)
+    g.both(y,None,lambda n: own(n).start())
+    for e in g.events(): e()
+    g.finish()
+    g.both(y,None,lambda n: own(n).wait())
+    pl.when(y==1)(lambda: ecopy.wait_send())
+
+def gather_weights(master):
+    return pl.pallas_call(ag_kernel,out_shape=jax.ShapeDtypeStruct((9984,768),jnp.bfloat16),
+        in_specs=[pl.BlockSpec(memory_space=pltpu.VMEM)],out_specs=pl.BlockSpec(memory_space=pl.ANY),
+        scratch_shapes=[pltpu.VMEM((320,768),jnp.bfloat16),pltpu.VMEM((8,768),jnp.float32),pltpu.SemaphoreType.DMA((2,)),
+            pltpu.SemaphoreType.DMA((2,16,5)),pltpu.SemaphoreType.DMA((2,16)),pltpu.SemaphoreType.DMA((2,16)),pltpu.SemaphoreType.DMA],
+        compiler_params=pltpu.CompilerParams(collective_id=0,has_side_effects=True,vmem_limit_bytes=40<<20),name="gather_weights")(master)
+
+
 def local(
+    tuned,
     values,
     names,
     counts,
@@ -136,7 +273,10 @@
 ):
     row_count, row_span, width = values.shape
     token_count = row_count * row_span
-    weights = lax.all_gather(master.astype(jnp.bfloat16), ("seq", "batch"), axis=0, tiled=True)
+    if tuned:
+        weights = gather_weights(master)
+    else:
+        weights = lax.all_gather(master.astype(jnp.bfloat16), ("seq", "batch"), axis=0, tiled=True)
     w_qkv = weights[0 : 3 * D]
     w_attn = weights[3 * D : 4 * D]
     w_unite = weights[4 * D : 5 * D]
@@ -264,7 +404,7 @@
         ]
     )
     grads = jnp.concatenate([grad_w_qkv, grad_w_attn, grad_w_unite, grad_w_in, grad_w_down], axis=0)
-    owned = lax.psum_scatter(grads, ("seq", "batch"), scatter_dimension=0, tiled=True)
+    owned = lax.psum_scatter(grads.astype(jnp.bfloat16), ("seq", "batch"), scatter_dimension=0, tiled=True).astype(jnp.float32)
     local_squares = jnp.sum(owned * owned)
     vector_total, matrix_squares = lax.psum((vector_grads, local_squares), ("seq", "batch"))
     grad_norm = jnp.sqrt(matrix_squares + jnp.sum(vector_total * vector_total))
@@ -291,8 +431,9 @@
 
 
 def solution(mesh):
+    tuned = dict(mesh.shape) == {"seq": 4, "batch": 8}
     return jax.shard_map(
-        local,
+        functools.partial(local, tuned),
         mesh=mesh,
         in_specs=(
             P("batch", "seq", None),

time: 730 us -> 602 us (0.82)
  waiting for transfers between devices: 493 us -> 282 us
  Pallas kernels: 0 us -> 79 us
    all_gather x1 -> x0, waiting for transfers between devices: 110 us -> none  [local(): lax.all_gather(master.astype(jnp.bfloat16), ('seq', 'batch'), axis=0, til...]
    reduce_scatter x1, waiting for transfers between devices: 274 us -> 165 us  [local(): lax.psum_scatter(grads.astype(jnp.bfloat16), ('seq', 'batch'), scatter_di...]
    pallas_call x0 -> x1, Pallas kernels: none -> 79 us  [gather_weights(): pl.pallas_call(ag_kernel, out_shape=jax.ShapeDtypeStruct((9984, 768), jnp...]
    all_gather x1, waiting for transfers between devices: 13.4 us -> 26.5 us  [local(): lax.all_gather(key_proj, 'seq', axis=1, tiled=True)]
  transfers between devices with their start and end apart: 6 -> 5, of which waited for: 6 -> 5; matrix products, arithmetic and copies ran while one was open for 1% -> 1% of each run, Pallas kernels for 0% -> 0%
where the time goes in v1:
time: 602 us; the launch traced here: 594 us
  waiting for transfers between devices  282 us (47%)
  matrix products  90.5 us (15%)
  Pallas kernels  79 us (13%)
  local copies, waits for them, and re-layouts  58.5 us (10%)
  blocking collectives  45.3 us (8%)
  other arithmetic  21.1 us (4%)
  between operations  17.5 us (3%)
    reduce_scatter x1, waiting for transfers between devices, local(): lax.psum_scatter(grads.astype(jnp.bfloat16), ('seq', 'batch'), scatter_di...  165 us
    pallas_call x1, Pallas kernels, gather_weights(): pl.pallas_call(ag_kernel, out_shape=jax.ShapeDtypeStruct((9984, 768), jnp...  79 us
    psum x1, blocking collectives, local(): lax.psum((vector_grads, local_squares), ('seq', 'batch'))  40.1 us
    reduce_scatter x1, waiting for transfers between devices, local(): lax.psum_scatter(key_terms.reshape(row_count, -1, D).astype(jnp.bfloat16)...  36.2 us
    reduce_scatter x1, waiting for transfers between devices, local(): lax.psum_scatter(value_terms.reshape(row_count, -1, D).astype(jnp.bfloat1...  32.6 us
    dot_general x5, matrix products, matmul_t(): lax.dot_general(first_op, second_op, (((1,), (1,)), ((), ())), preferred_...  28.6 us
    all_gather x1, waiting for transfers between devices, local(): lax.all_gather(key_proj, 'seq', axis=1, tiled=True)  26.5 us
    dynamic_slice x21, local copies, waits for them, and re-layouts, local(): lax.map(attend_block, (blocked(query), blocked(key_all), blocked(value_al...  26.1 us
  transfers between devices with their start and end apart: 5, of which 5 were waited for; matrix products, arithmetic and copies ran while one was open for 1% of the time, Pallas kernels for 0%

profile of v1, /device:TPU:0, one launch (start us, length us, event | category | flops | bytes accessed | tf_op | source)
XLA Modules:
  0.0 594.3 jit_solution(2925826279262639237)
XLA Ops:
  9.4 79.0 %gather_weights.1 = bf16[9984,768]{1,0:T(8,128)(2,1)} custom-call(f32[312,768]{1,0:T(8,128)S(1)} %copy-done.2), custom_call_target="tpu_custom_call" | custom-call | tf_op jit(solution)/shard_map/gather_weights/pallas_call | solution.py:253
  90.1 1.9 convolution_add_fusion.2
  92.1 4.0 fusion.26
  96.1 1.8 copy-done.16
  101.7 5.3 all_gather.10
  108.1 20.3 %all-gather.3.cloned.1.call-done = bf16[3,512,768]{1,2,0:T(8,128)(2,1)} async-done(((bf16[3,128,768]{1,2,0:T(8,128)(2,1)}), bf16[3,512,768]{1,2,0:T(8,128)(2,1)}) %all-gather.3.cloned.1.call-update) | async-done | bytes 2359312 | tf_op jit(solution)/shard_map/all_gather | solution.py:313
  128.4 26.5 %all-gather.5.cloned.1.call-done = bf16[3,512,768]{1,2,0:T(8,128)(2,1)} async-done(((bf16[3,128,768]{1,2,0:T(8,128)(2,1)}), bf16[3,512,768]{1,2,0:T(8,128)(2,1)}) %all-gather.5.cloned.1.call-update) | async-done | bytes 2359312 | tf_op jit(solution)/shard_map/all_gather | solution.py:312
  154.9 18.6 %while.26 = (s32[]{:T(128)}, bf16[3,1,128,768]{3,2,0,1:T(8,128)(2,1)S(1)}, f32[3,1,12,128]{3,2,1,0:T(8,128)}, bf16[3,1,512,768]{2,3,1,0:T(8,128)(2,1)}, bf16[3,1...) while((s32[]{:T(128)}, ...), condition=%wide.region_4.5_spmd, body=%wide.region_1.4_spmd.sunk | while | flops 210861056 | bytes 15783025 | solution.py:322
  155.1 1.5 constant_dynamic-slice_fusion.14
  173.5 2.2 fusion.88
  176.1 15.2 %multiply_convert_fusion.1 = (bf16[384,3072]{1,0:T(8,128)(2,1)S(1)}, f32[384,3072]{1,0:T(8,128)}, f32[384,3072]{1,0:T(8,128)}) fusion(f32[3072]{0:T(1024)S(1)} %slice-done.4, bf16[9984,768]{1,0:T(8,128)(2,1)} %gather_weights.1, f32[384,768]{1,0:T(8,128)S(1)} %get-tuple-element.219, f32[768]{0:T(1024)S(1)} %get-tuple-element.212, ...), kind=kOutput, calls=%fused_computation.42 | convolution fusion | flops 1891270656 | bytes 17716224 | tf_op jit(solution)/shard_map/dot_general | solution.py:43
  191.4 2.1 fusion.89
  196.4 5.9 convert_reduce_fusion
  202.3 2.8 multiply_reduce_fusion.1
  205.8 1.5 convolution_convert_fusion.6
  207.3 67.3 %while.27 = (s32[]{:T(128)}, bf16[3,1,128,768]{3,2,0,1:T(8,128)(2,1)}, bf16[3,1,512,768]{3,2,0,1:T(8,128)(2,1)}, bf16[3,1,512,768]{3,2,0,1:T(8,128)(2,1)}, bf16[...) while((s32[]{:T(128)}, ...), condition=%wide.region_15.16_spmd, body=%wide.region_13.15_spmd.sunk | while | flops 511376384 | bytes 46260484 | solution.py:350
  211.3 1.6 constant_dynamic-slice_fusion.18
  216.0 1.7 multiply_convert_fusion.3
  217.7 2.8 convolution_multiply_fusion.4
  220.5 1.7 copy.76
  222.2 1.6 constant_dynamic-update-slice_fusion.17
  226.5 1.8 convolution_multiply_fusion.5
  233.8 1.6 constant_dynamic-slice_fusion.18
  238.4 1.7 multiply_convert_fusion.3
  240.1 2.8 convolution_multiply_fusion.4
  242.9 1.7 copy.76
  244.6 1.6 constant_dynamic-update-slice_fusion.17
  248.9 1.8 convolution_multiply_fusion.5
  256.2 1.6 constant_dynamic-slice_fusion.18
  260.8 1.7 multiply_convert_fusion.3
  262.6 2.8 convolution_multiply_fusion.4
  265.3 1.7 copy.76
  267.1 1.6 constant_dynamic-update-slice_fusion.17
  271.4 1.8 convolution_multiply_fusion.5
  275.3 32.6 %reduce-scatter.6.cloned.1.call-done = bf16[3,128,768]{2,1,0:T(8,128)(2,1)} async-done(((bf16[3,512,768]{2,1,0:T(8,128)(2,1)}), bf16[3,128,768]{2,1,0:T(8,128)(2,1)}) %reduce-scatter.6.cloned.1.call-update) | async-done | bytes 589840 | tf_op jit(solution)/shard_map/reduce_scatter | solution.py:368
  307.9 36.2 %reduce-scatter.4.cloned.1.call-done = bf16[3,128,768]{2,1,0:T(8,128)(2,1)} async-done(((bf16[3,512,768]{2,1,0:T(8,128)(2,1)}), bf16[3,128,768]{2,1,0:T(8,128)(2,1)}) %reduce-scatter.4.cloned.1.call-update) | async-done | bytes 589840 | tf_op jit(solution)/shard_map/reduce_scatter | solution.py:362
  344.2 4.1 fusion.39
  348.3 3.8 fusion.10
  352.2 1.8 fusion.30
  354.0 1.8 fusion.31
  355.9 4.9 fusion.9
  360.8 4.4 fusion.8
  366.5 1.9 convolution_convert_fusion.5
  368.7 165.3 %reduce-scatter.8.cloned.1.call-done = bf16[312,768]{1,0:T(8,128)(2,1)} async-done(((bf16[9984,768]{1,0:T(8,128)(2,1)}), bf16[312,768]{1,0:T(8,128)(2,1)}) %reduce-scatter.8.cloned.1.call-update) | async-done | bytes 479248 | tf_op jit(solution)/shard_map/reduce_scatter | solution.py:407
  534.0 1.9 fusion.62
  536.0 3.5 fusion.48
  539.6 40.1 %all-reduce = (f32[]{:T(128)}, f32[9216]{0:T(1024)S(1)}) all-reduce(f32[]{:T(128)} %fusion.62, f32[9216]{0:T(1024)S(1)} %constant_dynamic-update-slice_fusion.8), channel_id=1, replica_groups=mesh['seq'=4,'batch'=8] {'seq','batch'}, use_global_device_ids=true, to_apply=%region_20.21 | all-reduce | flops 9217 | bytes 73736 | tf_op jit(solution)/shard_map/psum | solution.py:409
  581.7 2.7 fusion.81
  (264 shorter events, 67.2 us)
Async XLA Ops:
  7.2 81.6 %copy-start = (bf16[3,384,768]{2,1,0:T(8,128)(2,1)S(1)}, bf16[3,384,768]{2,1,0:T(8,128)(2,1)}, u32[]{:S(2)}) copy-start(bf16[3,384,768]{2,1,0:T(8,128)(2,1)} %param.16) | copy-start | bytes 5308420
  7.2 121.2 %all-gather.3.cloned.1.call-start = ((), (), s32[]{:S(2)}) async-start(), calls=%async_computation.3 | async-start | bytes 2949120 | tf_op jit(solution)/shard_map/all_gather | solution.py:313
  9.4 182.0 %copy-start.44 = (f32[768]{0:T(1024)}, f32[768]{0:T(1024)S(1)}, u32[]{:S(2)}) copy-start(f32[768]{0:T(1024)S(1)} %get-tuple-element.212) | copy-start | bytes 9220
  9.4 195.8 %copy-start.36 = (f32[768]{0:T(1024)}, f32[768]{0:T(1024)S(1)}, u32[]{:S(2)}) copy-start(f32[768]{0:T(1024)S(1)} %get-tuple-element.213) | copy-start | bytes 9220
  9.4 79.0 %copy-start.35 = (s32[3,128]{1,0:T(4,128)S(1)}, s32[3,128]{1,0:T(4,128)}, u32[]{:S(2)}) copy-start(s32[3,128]{1,0:T(4,128)} %param.17) | copy-start | bytes 4612
  88.4 3.6 copy-start.51
  92.1 81.4 %copy-start.10 = (f32[384,768]{1,0:T(8,128)}, f32[384,768]{1,0:T(8,128)S(1)}, u32[]{:S(2)}) copy-start(f32[384,768]{1,0:T(8,128)S(1)} %convolution_add_fusion.2) | copy-start | bytes 3538948
  98.1 3.7 copy-start.50
  99.2 55.7 %all-gather.5.cloned.1.call-start = ((), (), s32[]{:S(2)}) async-start(), calls=%async_computation.4 | async-start | bytes 2949120 | tf_op jit(solution)/shard_map/all_gather | solution.py:312
  101.6 206.3 %reduce-scatter.6.cloned.1.call-start = ((), (), s32[]{:S(2)}) async-start(), calls=%async_computation.6 | async-start | bytes 2949120 | tf_op jit(solution)/shard_map/reduce_scatter | solution.py:368
  173.5 17.8 %copy-start.21 = (bf16[3,1,128,768]{3,2,0,1:T(8,128)(2,1)}, bf16[3,1,128,768]{3,2,0,1:T(8,128)(2,1)S(1)}, u32[]{:S(2)}) copy-start(bf16[3,1,128,768]{3,2,0,1:T(8,128)(2,1)S(1)} %get-tuple-element.103) | copy-start | bytes 1769476
  173.5 17.8 %slice-start = ((s8[15335424]{0:T(1024)(128)(4,1)}), s8[4194304]{0:T(1024)(128)(4,1)S(1)}, s32[]{:S(2)}) async-start(s8[15335424]{0:T(1024)(128)(4,1)} %bitcast.153), calls=%async_computation.8 | async-start | bytes 8388608
  175.7 29.4 %copy-start.6 = (f32[384,768]{1,0:T(8,128)}, f32[384,768]{1,0:T(8,128)S(1)}, u32[]{:S(2)}) copy-start(f32[384,768]{1,0:T(8,128)S(1)} %get-tuple-element.219) | copy-start | bytes 3538948
  176.0 29.1 %copy-start.39 = (f32[384]{0:T(512)}, f32[384]{0:T(512)S(1)}, u32[]{:S(2)}) copy-start(f32[384]{0:T(512)S(1)} %fusion.75) | copy-start | bytes 4612
  176.1 15.3 %slice-start.1 = ((s8[15335424]{0:T(1024)(128)(4,1)}), s8[4194304]{0:T(1024)(128)(4,1)S(1)}, s32[]{:S(2)}) async-start(s8[15335424]{0:T(1024)(128)(4,1)} %bitcast.153), calls=%async_computation.9 | async-start | bytes 8388608
  176.1 15.3 %slice-start.2 = ((s8[15335424]{0:T(1024)(128)(4,1)}), s8[4194304]{0:T(1024)(128)(4,1)S(1)}, s32[]{:S(2)}) async-start(s8[15335424]{0:T(1024)(128)(4,1)} %bitcast.153), calls=%async_computation.10 | async-start | bytes 8388608
  176.1 15.3 %slice-start.3 = ((s8[15335424]{0:T(1024)(128)(4,1)}), s8[2752512]{0:T(1024)(128)(4,1)S(1)}, s32[]{:S(2)}) async-start(s8[15335424]{0:T(1024)(128)(4,1)} %bitcast.153), calls=%async_computation.11 | async-start | bytes 5505024
  195.9 6.3 %copy-start.26 = (bf16[384,768]{1,0:T(8,128)(2,1)}, bf16[384,768]{1,0:T(8,128)(2,1)S(1)}, u32[]{:S(2)}) copy-start(bf16[384,768]{1,0:T(8,128)(2,1)S(1)} %get-tuple-element.190) | copy-start | bytes 1769476
  207.3 4.0 copy-start.31
  229.8 4.0 copy-start.31
  252.2 4.0 copy-start.31
  274.7 69.5 %copy-start.13 = (f32[384,768]{1,0:T(8,128)S(1)}, f32[384,768]{1,0:T(8,128)}, u32[]{:S(2)}) copy-start(f32[384,768]{1,0:T(8,128)} %copy-done.12) | copy-start | bytes 3538948
  274.7 69.5 %copy-start.24 = (bf16[3,1,128,768]{3,2,0,1:T(8,128)(2,1)S(1)}, bf16[3,1,128,768]{3,2,0,1:T(8,128)(2,1)}, u32[]{:S(2)}) copy-start(bf16[3,1,128,768]{3,2,0,1:T(8,128)(2,1)} %get-tuple-element.105) | copy-start | bytes 1769476
  274.7 69.5 %reduce-scatter.4.cloned.1.call-start = ((), (), s32[]{:S(2)}) async-start(), calls=%async_computation.5 | async-start | bytes 2949120 | tf_op jit(solution)/shard_map/reduce_scatter | solution.py:362
  275.3 258.8 %reduce-scatter.8.cloned.1.call-start = ((), (), s32[]{:S(2)}) async-start(), calls=%async_computation.7 | async-start | bytes 15814656 | tf_op jit(solution)/shard_map/reduce_scatter | solution.py:407
  344.2 4.1 copy-start.11
  344.2 4.1 copy-start.25
  344.2 4.1 copy-start.53
  348.3 18.2 %copy-start.14 = (f32[384,768]{1,0:T(8,128)}, f32[384,768]{1,0:T(8,128)S(1)}, u32[]{:S(2)}) copy-start(f32[384,768]{1,0:T(8,128)S(1)} %fusion.39) | copy-start | bytes 3538948
  348.3 3.8 copy-start.22
  348.3 3.8 copy-start.29
  352.1 3.7 copy-start.7
  352.1 3.7 copy-start.37
  352.2 3.7 copy-start.40
  352.2 3.7 copy-start.45
  352.2 3.7 copy-start.57
  355.9 4.9 copy-start.27
  355.9 4.9 copy-start.55
  365.2 3.4 copy-start.38
  365.2 170.8 %copy-start.42 = (s32[3,128]{1,0:T(4,128)S(1)}, s32[3,128]{1,0:T(4,128)}, u32[]{:S(2)}) copy-start(s32[3,128]{1,0:T(4,128)} %copy-done.41) | copy-start | bytes 4612
  365.3 170.7 %copy-start.49 = (s32[3,128]{1,0:T(4,128)S(1)}, s32[3,128]{1,0:T(4,128)}, u32[]{:S(2)}) copy-start(s32[3,128]{1,0:T(4,128)} %copy-done.48) | copy-start | bytes 4612
  365.3 170.7 %copy-start.52 = (f32[3,128]{1,0:T(4,128)S(1)}, f32[3,128]{1,0:T(4,128)}, u32[]{:S(2)}) copy-start(f32[3,128]{1,0:T(4,128)} %copy-done.51) | copy-start | bytes 4612
  368.4 213.2 %copy-start.3 = (f32[312,768]{1,0:T(8,128)S(1)}, f32[312,768]{1,0:T(8,128)}, u32[]{:S(2)}) copy-start(f32[312,768]{1,0:T(8,128)} %master.1) | copy-start | bytes 2875396
  534.0 47.6 %copy-start.19 = (bf16[312,768]{1,0:T(8,128)(2,1)S(1)}, bf16[312,768]{1,0:T(8,128)(2,1)}, u32[]{:S(2)}) copy-start(bf16[312,768]{1,0:T(8,128)(2,1)} %reduce-scatter.8.cloned.1.call-done) | copy-start | bytes 1437700
  581.6 4.7 copy-start.1
  581.6 3.9 copy-start.30
  581.7 3.9 copy-start.33
  581.7 3.9 copy-start.34
  (29 other events, 64.9 us)
Sparse Core Ops, SparseCore 0:
  99.3 29.0 all-gather.2
  130.5 24.3 all-gather.4
  274.8 33.0 reduce-scatter.5
  311.1 33.0 reduce-scatter.3
  365.3 168.6 reduce-scatter.7

commit v2 on v0

--- a/solution.py
+++ b/solution.py
@@ -1,9 +1,14 @@
+import functools
 import math
 
 import jax
 import jax.numpy as jnp
 from jax import lax
+from jax.experimental import pallas as pl
+from jax.experimental.pallas import tpu as pltpu
 from jax.sharding import PartitionSpec as P
+
+MESH = pl.DeviceIdType.MESH
 
 D = 768
 HEAD = 64
@@ -119,6 +124,489 @@
     new_weight = weight - rate * (clipped + momentum_decay * new_moment)
     new_mean = average_decay * mean_state + (1.0 - average_decay) * new_weight
     return (new_weight, new_moment, new_mean)
+
+
+def place():
+    s = lax.axis_index("seq")
+    b = lax.axis_index("batch")
+    return s // 2, s % 2, b // 2, b % 2
+
+
+def when(cond, fn):
+    if cond is None:
+        fn()
+    else:
+        pl.when(cond)(fn)
+
+
+def both_of(first, second):
+    if first is None:
+        return second
+    if second is None:
+        return first
+    return jnp.logical_and(first, second)
+
+
+def by_size(y0, cond, fn):
+    if isinstance(y0, int):
+        when(cond, lambda: fn(320 if y0 == 0 else 304))
+    else:
+        when(both_of(y0 == 0, cond), lambda: fn(320))
+        when(both_of(y0 == 1, cond), lambda: fn(304))
+
+
+def neighbour(d):
+    x, c, z, y = place()
+    if d == "x":
+        return {"seq": (1 - x) * 2 + c, "batch": z * 2 + y}
+    if d == "y":
+        return {"seq": x * 2 + c, "batch": z * 2 + 1 - y}
+    if d == "c":
+        return {"seq": x * 2 + 1 - c, "batch": z * 2 + y}
+    if d == "u":
+        return {"seq": x * 2 + c, "batch": jnp.minimum(z + 1, 3) * 2 + y}
+    return {"seq": x * 2 + c, "batch": jnp.maximum(z - 1, 0) * 2 + y}
+
+
+def piece_rows(x0, c, z0, y0, rows):
+    return pl.ds(pl.multiple_of((2 * x0 + c) * 2496 + z0 * 624 + 320 * y0, 16), rows)
+
+
+def piece_id(x0, z0, y0):
+    return x0 * 8 + z0 * 2 + y0
+
+
+COLS = ((0, 512), (512, 256))
+
+
+def entry_barrier():
+    x, c, z, y = place()
+    bar = pltpu.get_barrier_semaphore()
+    for d, cond in (("x", None), ("y", None), ("c", None), ("u", z < 3), ("d", z > 0)):
+        when(
+            cond,
+            lambda d=d: pl.semaphore_signal(bar, 1, device_id=neighbour(d), device_id_type=MESH),
+        )
+    pl.semaphore_wait(bar, 3 + (z < 3).astype(jnp.int32) + (z > 0).astype(jnp.int32))
+
+
+class Gather:
+    def __init__(self, weights, stage, send_sem, recv_sem, pair_sem):
+        self.weights, self.stage = weights, stage
+        self.send_sem, self.recv_sem, self.pair_sem = send_sem, recv_sem, pair_sem
+        self.sent = []
+
+    def copy(self, t, x0, z0, y0, d, rows, own):
+        c = place()[1]
+        cols = pl.ds(*COLS[t])
+        dst = self.weights.at[piece_rows(x0, c, z0, y0, rows), cols]
+        src = self.stage.at[pl.ds(0, rows), cols] if own else dst
+        k = piece_id(x0, z0, y0)
+        way = {"u": 0, "d": 1, "x": 2 if t else 4, "y": 4 if t else 2, "c": 3}[d]
+        return pltpu.make_async_remote_copy(
+            src_ref=src,
+            dst_ref=dst,
+            send_sem=self.send_sem.at[t, k, way],
+            recv_sem=(self.pair_sem if d == "c" else self.recv_sem).at[t, k],
+            device_id=neighbour(d),
+            device_id_type=MESH,
+        )
+
+    def send(self, t, x0, z0, y0, ways, own=False, cond=None):
+        for d, way_cond in ways:
+            whole = both_of(way_cond, cond)
+            by_size(y0, whole, lambda rows, d=d: self.copy(t, x0, z0, y0, d, rows, own).start())
+            self.sent.append((t, x0, z0, y0, d, own, whole))
+
+    def recv(self, t, x0, z0, y0, cond=None):
+        by_size(y0, cond, lambda rows: self.copy(t, x0, z0, y0, "x", rows, False).wait_recv())
+
+    def start(self):
+        x, c, z, y = place()
+        line = [("u", z < 3), ("d", z > 0), ("c", None)]
+        self.send(0, x, z, y, [("x", None), ("y", None)] + line, own=True)
+        self.send(1, x, z, y, [("y", None), ("x", None)] + line, own=True)
+
+    def steps(self, g):
+        x, c, z, y = place()
+        up, down = z < 3, z > 0
+        here, there = x == g, x == 1 - g
+
+        def first():
+            self.recv(0, g, z, y, cond=there)
+            ways = [("u", up), ("d", down), ("y", None), ("c", None)]
+            self.send(0, g, z, y, ways, cond=there)
+            self.recv(1, g, z, 1 - y, cond=here)
+            ways = [("u", up), ("d", down), ("x", None), ("c", None)]
+            self.send(1, g, z, 1 - y, ways, cond=here)
+
+        def along(d, sign):
+            z0 = z + sign * d
+            inside = (z0 >= 0) if sign < 0 else (z0 <= 3)
+            relay = ("u", up) if sign < 0 else ("d", down)
+            self.recv(0, g, z0, y, cond=inside)
+            self.send(0, g, z0, y, [relay, ("y", None), ("c", None)], cond=inside)
+            for flip in (0, 1):
+                y0 = y if flip == 0 else 1 - y
+                self.recv(1, g, z0, y0, cond=both_of(inside, here))
+                ways = [relay, ("x", None), ("c", None)]
+                self.send(1, g, z0, y0, ways, cond=both_of(inside, here))
+
+        def leaf(z0):
+            self.recv(0, g, z0, 1 - y)
+            self.send(0, g, z0, 1 - y, [("c", None)])
+            for y0 in (0, 1):
+                self.recv(1, g, z0, y0, cond=there)
+                self.send(1, g, z0, y0, [("c", None)], cond=there)
+
+        out = [first]
+        for d in (1, 2, 3):
+            for sign in (-1, 1):
+                out.append(functools.partial(along, d, sign))
+        for z0 in range(4):
+            out.append(functools.partial(leaf, z0))
+        return out
+
+    def pair_wait(self, g):
+        c = place()[1]
+        for t in (0, 1):
+            for z0 in range(4):
+                for y0 in (0, 1):
+                    rows = 320 if y0 == 0 else 304
+                    ref = self.weights.at[piece_rows(g, 1 - c, z0, y0, rows), pl.ds(*COLS[t])]
+                    k = piece_id(g, z0, y0)
+                    pltpu.make_async_remote_copy(
+                        src_ref=ref,
+                        dst_ref=ref,
+                        send_sem=self.send_sem.at[t, k, 0],
+                        recv_sem=self.pair_sem.at[t, k],
+                        device_id=neighbour("c"),
+                        device_id_type=MESH,
+                    ).wait_recv()
+
+    def finish(self):
+        for t, x0, z0, y0, d, own, cond in self.sent:
+            by_size(
+                y0, cond, lambda rows: self.copy(t, x0, z0, y0, d, rows, own).wait_send()
+            )
+
+
+def dot(first_op, second_op):
+    return lax.dot_general(
+        first_op, second_op, (((1,), (0,)), ((), ())), preferred_element_type=jnp.float32
+    )
+
+
+def dot_t(first_op, second_op):
+    return lax.dot_general(
+        first_op, second_op, (((1,), (1,)), ((), ())), preferred_element_type=jnp.float32
+    )
+
+
+def t_dot(first_op, second_op):
+    return lax.dot_general(
+        first_op, second_op, (((0,), (0,)), ((), ())), preferred_element_type=jnp.float32
+    )
+
+
+def stack_heads(two):
+    lane = lax.broadcasted_iota(jnp.int32, two.shape, 1)
+    none = jnp.zeros_like(two)
+    return jnp.concatenate([jnp.where(lane < 64, two, none), jnp.where(lane < 64, none, two)], axis=0)
+
+
+def unstack_heads(stacked):
+    half = stacked.shape[0] // 2
+    lane = lax.broadcasted_iota(jnp.int32, (half, stacked.shape[1]), 1)
+    return jnp.where(lane < 64, stacked[:half], stacked[half:])
+
+
+def attend_row(r, q_ref, k_ref, v_ref, bias, ctx_ref, lse_ref):
+    for pair in range(6):
+        lanes = pl.ds(pair * 128, 128)
+        scores = dot_t(k_ref[r, :, lanes], stack_heads(q_ref[r, :, lanes])) + bias
+        top = jnp.max(scores, axis=0, keepdims=True)
+        exps = jnp.exp(scores - top)
+        total = jnp.sum(exps, axis=0, keepdims=True)
+        prob = (exps * (1.0 / total)).astype(jnp.bfloat16)
+        ctx_ref[r, :, lanes] = unstack_heads(t_dot(prob, v_ref[r, :, lanes])).astype(jnp.bfloat16)
+        lse = top + jnp.log(total)
+        lse_ref[r, 2 * pair : 2 * pair + 1, :] = lse[:, :128]
+        lse_ref[r, 2 * pair + 1 : 2 * pair + 2, :] = lse[:, 128:]
+
+
+def norm_rows(z):
+    centre = jnp.mean(z, axis=-1, keepdims=True)
+    centred = z - centre
+    spread = jnp.mean(centred * centred, axis=-1, keepdims=True)
+    scale = lax.rsqrt(spread + norm_eps)
+    return centred * scale, scale
+
+
+def norm_back_rows(e, gain, zhat, scale):
+    a = e * gain
+    mean_a = jnp.mean(a, axis=-1, keepdims=True)
+    mean_az = jnp.mean(a * zhat, axis=-1, keepdims=True)
+    return (a - mean_a - zhat * mean_az) * scale
+
+
+def forward_kernel(
+    master, values, names, slots, valid, vecs, b_in, out_grad,
+    w_out, first_out, pooled_out, q_out, k_out, v_out, valid_out, ctx_out, lse_out,
+    zhat_out, scale_out, hidden_out, slope_out, output_out, two_out, vec_out,
+    weights, stage, edge, first, pooled, united, q, k, v, valid_all, ctx, lse,
+    zhat, scale, hidden, slope, output, two, vec_grad,
+    edge_sem, send_sem, recv_sem, pair_sem, kv_send, kv_recv, valid_sem, out_sem,
+):
+    x, c, z, y = place()
+    me = 2 * x + c
+    gather = Gather(weights, stage, send_sem, recv_sem, pair_sem)
+    entry_barrier()
+    edge_copy = pltpu.make_async_remote_copy(
+        src_ref=master.at[pl.ds(0, 8)],
+        dst_ref=edge,
+        send_sem=edge_sem.at[0],
+        recv_sem=edge_sem.at[1],
+        device_id=neighbour("y"),
+        device_id_type=MESH,
+    )
+
+    @pl.when(y == 1)
+    def _():
+        edge_copy.start()
+        stage[0:304] = master[8:312].astype(jnp.bfloat16)
+        stage[304:320] = jnp.zeros((16, D), jnp.bfloat16)
+
+    @pl.when(y == 0)
+    def _():
+        stage[0:304] = master[0:304].astype(jnp.bfloat16)
+        edge_copy.wait_recv()
+        stage[304:320] = jnp.concatenate([master[304:312], edge[...]], axis=0).astype(jnp.bfloat16)
+
+    gather.start()
+
+    def own(rows):
+        return pltpu.make_async_copy(
+            stage.at[pl.ds(0, rows)], weights.at[piece_rows(x, c, z, y, rows)], edge_sem.at[2]
+        )
+
+    by_size(y, None, lambda rows: own(rows).start())
+
+    valid_all[me] = valid[...]
+
+    def valid_copy(where, d, slot):
+        return pltpu.make_async_remote_copy(
+            src_ref=valid_all.at[where],
+            dst_ref=valid_all.at[where],
+            send_sem=valid_sem.at[0, slot],
+            recv_sem=valid_sem.at[1, slot],
+            device_id=neighbour(d),
+            device_id_type=MESH,
+        )
+
+    valid_copy(me, "x", 0).start()
+    valid_copy(me, "c", 1).start()
+
+    for r in range(3):
+        rows = pl.ds(r * 128, 128)
+        begin, end = slots[rows, 0:1], slots[rows, 1:2]
+        slot_id = lax.broadcasted_iota(jnp.int32, (128, NAME_DEV), 1)
+        inside = jnp.logical_and(slot_id >= begin, slot_id < end).astype(jnp.float32)
+        divisor = jnp.maximum((end - begin).astype(jnp.float32), 1.0)
+        summed = dot(inside.astype(jnp.bfloat16), names[r])
+        pooled[rows] = (summed / divisor).astype(jnp.bfloat16)
+
+    for step in gather.steps(0):
+        step()
+    by_size(y, None, lambda rows: own(rows).wait())
+    gather.pair_wait(0)
+
+    for j in range(3):
+        cols = pl.ds(j * 256, 256)
+        tile = values[:, cols].astype(jnp.float32) + dot(pooled[...], weights[4 * D : 5 * D, cols])
+        united[:, cols] = tile
+        first[:, cols] = tile.astype(jnp.bfloat16)
+    here = pl.ds(pl.multiple_of(me * 128, 128), 128)
+
+    def project(base):
+        return dot_t(first[...], weights[pl.ds(base, 256)])
+
+    for j in range(3):
+        cols = pl.ds(j * 256, 256)
+        tile = project(D + j * 256).astype(jnp.bfloat16)
+        for r in range(3):
+            k[r, here, cols] = tile[r * 128 : (r + 1) * 128]
+        tile = (project(2 * D + j * 256) + vecs[1:2, cols]).astype(jnp.bfloat16)
+        for r in range(3):
+            v[r, here, cols] = tile[r * 128 : (r + 1) * 128]
+
+    def kv_copy(r, which, where, d, slot):
+        at = (k if which == 0 else v).at[r, pl.ds(pl.multiple_of(where * 128, 128), 128)]
+        return pltpu.make_async_remote_copy(
+            src_ref=at,
+            dst_ref=at,
+            send_sem=kv_send.at[r, which, slot],
+            recv_sem=kv_recv.at[r, which, slot],
+            device_id=neighbour(d),
+            device_id_type=MESH,
+        )
+
+    for r in range(3):
+        for which in (0, 1):
+            kv_copy(r, which, me, "x", 0).start()
+            kv_copy(r, which, me, "c", 1).start()
+    across, beside, corner = 2 * (1 - x) + c, 2 * x + 1 - c, 2 * (1 - x) + 1 - c
+    valid_copy(across, "x", 0).wait_recv()
+    valid_copy(across, "c", 2).start()
+    for j in range(3):
+        cols = pl.ds(j * 256, 256)
+        tile = (project(j * 256) + vecs[0:1, cols]).astype(jnp.bfloat16)
+        tile = (tile.astype(jnp.float32) * 0.125).astype(jnp.bfloat16)
+        for r in range(3):
+            q[r, :, cols] = tile[r * 128 : (r + 1) * 128]
+
+    rest = gather.steps(1)
+    cut = [rest[:5], rest[5:8], rest[8:]]
+    valid_copy(beside, "c", 1).wait_recv()
+    valid_copy(corner, "c", 2).wait_recv()
+    biases = jnp.concatenate([valid_all[i] for i in range(4)], axis=1)
+    bias_cols = jnp.transpose(biases)
+    for r in range(3):
+        for step in cut[r]:
+            step()
+        for which in (0, 1):
+            kv_copy(r, which, across, "x", 0).wait_recv()
+            kv_copy(r, which, across, "c", 2).start()
+        for which in (0, 1):
+            kv_copy(r, which, beside, "c", 1).wait_recv()
+            kv_copy(r, which, corner, "c", 2).wait_recv()
+        attend_row(r, q, k, v, bias_cols[:, r : r + 1], ctx, lse)
+
+    outs = []
+
+    def emit(src, dst):
+        copy = pltpu.make_async_copy(src, dst, out_sem.at[len(outs)])
+        copy.start()
+        outs.append(copy)
+
+    emit(first, first_out)
+    emit(pooled, pooled_out)
+    emit(q, q_out)
+    emit(k, k_out)
+    emit(v, v_out)
+    emit(valid_all, valid_out)
+    emit(ctx, ctx_out)
+    emit(lse, lse_out)
+    gather.pair_wait(1)
+    emit(weights, w_out)
+
+    for r in range(3):
+        rows = pl.ds(r * 128, 128)
+        attn_out = dot(ctx[r], weights[3 * D : 4 * D]) + vecs[2:3]
+        hat, rscale = norm_rows(united[rows] + attn_out)
+        zhat[rows] = hat
+        scale[rows] = jnp.broadcast_to(rscale, (128, 128))
+        normed = hat * vecs[3:4] + vecs[4:5]
+        united[rows] = normed
+        first_low = normed.astype(jnp.bfloat16)
+        stage_rows = pl.ds(r * 128, 128)
+        output[stage_rows] = first_low
+    emit(zhat, zhat_out)
+    emit(scale, scale_out)
+
+    def up_tile(j, carry):
+        w_tile = weights[pl.ds(pl.multiple_of(5 * D + j * 256, 256), 256)]
+        up = dot_t(output[...], w_tile) + b_in[pl.ds(j, 1)]
+        below = 0.5 + 0.5 * lax.erf(up * (0.5**0.5))
+        density = jnp.exp(-0.5 * up * up) * (1.0 / (2.0 * math.pi) ** 0.5)
+        cols = pl.ds(pl.multiple_of(j * 256, 256), 256)
+        hidden[:, cols] = (up * below).astype(jnp.bfloat16)
+        slope[:, cols] = (below + up * density).astype(jnp.bfloat16)
+        return carry
+
+    lax.fori_loop(0, FF // 256, up_tile, 0)
+    emit(hidden, hidden_out)
+    emit(slope, slope_out)
+
+    grad_gain = jnp.zeros((1, D), jnp.float32)
+    grad_shift = jnp.zeros((1, D), jnp.float32)
+    for j in range(3):
+        cols = pl.ds(j * 256, 256)
+        two[:, cols] = (
+            dot(hidden[...], weights[5 * D + FF : 5 * D + 2 * FF, cols])
+            + vecs[5:6, cols]
+            + united[:, cols]
+        )
+    for r in range(3):
+        rows = pl.ds(r * 128, 128)
+        hat, rscale = norm_rows(two[rows])
+        output[rows] = (hat * vecs[6:7] + vecs[7:8]).astype(jnp.bfloat16)
+        e = out_grad[rows].astype(jnp.float32)
+        grad_gain += jnp.sum(e * hat, axis=0, keepdims=True)
+        grad_shift += jnp.sum(e, axis=0, keepdims=True)
+        two[rows] = norm_back_rows(e, vecs[6:7], hat, rscale)
+    vec_grad[...] = jnp.zeros((8, D), jnp.float32)
+    vec_grad[0:1] = grad_gain
+    vec_grad[1:2] = grad_shift
+    emit(output, output_out)
+    emit(two, two_out)
+    emit(vec_grad, vec_out)
+
+    valid_copy(me, "x", 0).wait_send()
+    valid_copy(me, "c", 1).wait_send()
+    valid_copy(across, "c", 2).wait_send()
+    for r in range(3):
+        for which in (0, 1):
+            kv_copy(r, which, me, "x", 0).wait_send()
+            kv_copy(r, which, me, "c", 1).wait_send()
+            kv_copy(r, which, across, "c", 2).wait_send()
+    gather.finish()
+    pl.when(y == 1)(lambda: edge_copy.wait_send())
+    for copy in outs:
+        copy.wait()
+
+
+def forward_call(master, values, names, slots, valid, vecs, b_in, out_grad):
+    bf, f32 = jnp.bfloat16, jnp.float32
+    kept = [
+        ((9984, D), bf),
+        ((384, D), bf),
+        ((384, D), bf),
+        ((3, 128, D), bf),
+        ((3, 512, D), bf),
+        ((3, 512, D), bf),
+        ((4, 8, 128), f32),
+        ((3, 128, D), bf),
+        ((3, 16, 128), f32),
+        ((384, D), f32),
+        ((384, 128), f32),
+        ((384, FF), bf),
+        ((384, FF), bf),
+        ((384, D), bf),
+        ((384, D), f32),
+        ((8, D), f32),
+    ]
+    vmem = pl.BlockSpec(memory_space=pltpu.VMEM)
+    held = [pltpu.VMEM(shape, kind) for shape, kind in kept]
+    scratch = (
+        [held[0], pltpu.VMEM((320, D), bf), pltpu.VMEM((8, D), f32), held[1], held[2]]
+        + [pltpu.VMEM((384, D), f32)]
+        + held[3:]
+    )
+    dma = pltpu.SemaphoreType.DMA
+    sems = [dma((3,)), dma((2, 16, 5)), dma((2, 16)), dma((2, 16)), dma((3, 2, 3)), dma((3, 2, 3)), dma((2, 3)), dma((16,))]
+    return pl.pallas_call(
+        forward_kernel,
+        out_shape=[jax.ShapeDtypeStruct(shape, kind) for shape, kind in kept],
+        in_specs=[vmem] * 8,
+        out_specs=[pl.BlockSpec(memory_space=pl.ANY)] * len(kept),
+        scratch_shapes=scratch + sems,
+        compiler_params=pltpu.CompilerParams(
+            collective_id=0, has_side_effects=True, vmem_limit_bytes=58 << 20
+        ),
+        cost_estimate=pl.CostEstimate(flops=8 * 10**9, bytes_accessed=60 * 10**6, transcendentals=4 * 10**6),
+        name="gather_and_forward",
+    )(master, values, names, slots, valid, vecs, b_in, out_grad)
 
 
 def local(
@@ -290,9 +778,139 @@
     )
 
 
+def tuned(
+    values,
+    names,
+    counts,
+    valid,
+    out_grad,
+    master,
+    momentum,
+    average,
+    vectors,
+    vector_momentum,
+    vector_average,
+):
+    row_count, row_span, width = values.shape
+    token_count = row_count * row_span
+    slot_ends = jnp.cumsum(counts, axis=1)
+    slot_starts = slot_ends - counts
+    slots = jnp.stack([slot_starts.reshape(-1), slot_ends.reshape(-1)], axis=1)
+    masked = jnp.where(valid > 0, 0.0, big_negative).astype(jnp.float32)
+    masked = jnp.concatenate([masked, jnp.zeros((5, 128), jnp.float32)], axis=0)
+    vecs = jnp.concatenate([vectors[: 8 * D].reshape(8, D)], axis=0)
+    b_in = vectors[8 * D :].reshape(12, 256)
+    (weights, first, pooled, q, k, v, valid_all, context, lse, zhat, scale, hidden, slope,
+     output, grad_two, vec_grad) = forward_call(
+        master, values.reshape(token_count, D), names, slots, masked, vecs, b_in, out_grad.reshape(token_count, D))
+    w_qkv = weights[0 : 3 * D]
+    w_attn = weights[3 * D : 4 * D]
+    w_unite = weights[4 * D : 5 * D]
+    w_in = weights[5 * D : 5 * D + FF]
+    w_down = weights[5 * D + FF : 5 * D + 2 * FF]
+    gain_one = vectors[3 * D : 4 * D]
+    shift_one = vectors[4 * D : 5 * D]
+    slot_ids = jnp.arange(NAME_DEV, dtype=jnp.int32)
+    inside = (slot_ids >= slot_starts[:, :, None]) & (slot_ids < slot_ends[:, :, None])
+    divisor = jnp.maximum(counts.astype(jnp.float32), 1.0)[:, :, None]
+    context = context.reshape(token_count, D)
+    lowered = (zhat * gain_one + shift_one).astype(jnp.bfloat16)
+    grad_down = grad_two.astype(jnp.bfloat16)
+    grad_bias_down = jnp.sum(grad_down.astype(jnp.float32), axis=0)
+    grad_w_down = tokens_t(hidden, grad_down)
+    grad_hidden = matmul_t(grad_down, w_down)
+    grad_up = (grad_hidden * slope.astype(jnp.float32)).astype(jnp.bfloat16)
+    grad_bias_in = jnp.sum(grad_up.astype(jnp.float32), axis=0)
+    grad_w_in = tokens_t(grad_up, lowered)
+    e_one = grad_two + matmul(grad_up, w_in)
+    grad_gain_one = jnp.sum(e_one * zhat, axis=0)
+    grad_shift_one = jnp.sum(e_one, axis=0)
+    grad_one = norm_back_rows(e_one, gain_one, zhat, scale[:, 0:1])
+    grad_attn = grad_one.astype(jnp.bfloat16)
+    grad_bias_o = jnp.sum(grad_attn.astype(jnp.float32), axis=0)
+    grad_w_attn = tokens_t(context, grad_attn)
+    grad_context = matmul_t(grad_attn, w_attn).astype(jnp.bfloat16).reshape(row_count, row_span, D)
+    mask_all = (valid_all[:, :3].transpose(1, 0, 2).reshape(3, 512) == 0).astype(jnp.bfloat16)
+    grad_query, key_terms, value_terms = attend_back(
+        ((q.astype(jnp.float32) * 8).astype(jnp.bfloat16), k, v, mask_all, lse[:, :12], grad_context))
+    grad_key, grad_value = (
+        lax.psum_scatter(
+            key_terms.reshape(row_count, -1, D).astype(jnp.bfloat16),
+            "seq",
+            scatter_dimension=1,
+            tiled=True,
+        ).astype(jnp.float32),
+        lax.psum_scatter(
+            value_terms.reshape(row_count, -1, D).astype(jnp.bfloat16),
+            "seq",
+            scatter_dimension=1,
+            tiled=True,
+        ).astype(jnp.float32),
+    )
+    grad_q = grad_query.reshape(token_count, D).astype(jnp.bfloat16)
+    grad_k = grad_key.reshape(token_count, D).astype(jnp.bfloat16)
+    grad_v = grad_value.reshape(token_count, D).astype(jnp.bfloat16)
+    grad_bias_q = jnp.sum(grad_q.astype(jnp.float32), axis=0)
+    grad_bias_v = jnp.sum(grad_v.astype(jnp.float32), axis=0)
+    grad_qkv = jnp.concatenate([grad_q, grad_k, grad_v], axis=1)
+    grad_w_qkv = tokens_t(grad_qkv, first)
+    grad_united = grad_one + matmul(grad_qkv, w_qkv)
+    grad_unite = grad_united.astype(jnp.bfloat16)
+    grad_w_unite = tokens_t(pooled, grad_unite)
+    grad_pooled = lax.optimization_barrier(
+        matmul_t(grad_unite, w_unite).astype(jnp.bfloat16)
+    ).astype(jnp.float32)
+    grad_pooled = grad_pooled.reshape(row_count, row_span, D) / divisor
+    grad_names = jnp.einsum(
+        "rtn,rtd->rnd", inside.astype(jnp.float32), grad_pooled, precision=lax.Precision.HIGHEST
+    )
+    grad_values = grad_united.reshape(row_count, row_span, D)
+    vector_grads = jnp.concatenate(
+        [
+            grad_bias_q,
+            grad_bias_v,
+            grad_bias_o,
+            grad_gain_one,
+            grad_shift_one,
+            grad_bias_down,
+            vec_grad[0],
+            vec_grad[1],
+            grad_bias_in,
+        ]
+    )
+    grads = jnp.concatenate([grad_w_qkv, grad_w_attn, grad_w_unite, grad_w_in, grad_w_down], axis=0)
+    owned = lax.psum_scatter(
+        grads.astype(jnp.bfloat16), ("seq", "batch"), scatter_dimension=0, tiled=True
+    ).astype(jnp.float32)
+    local_squares = jnp.sum(owned * owned)
+    vector_total, matrix_squares = lax.psum((vector_grads, local_squares), ("seq", "batch"))
+    grad_norm = jnp.sqrt(matrix_squares + jnp.sum(vector_total * vector_total))
+    clip_factor = 1.0 / jnp.maximum(grad_norm, 1.0)
+    new_master, new_momentum, new_average = apply_update(
+        master, momentum, average, owned, clip_factor, step_rate
+    )
+    new_vectors, new_vector_momentum, new_vector_average = apply_update(
+        vectors, vector_momentum, vector_average, vector_total, clip_factor, vector_rate
+    )
+    return (
+        output.reshape(values.shape),
+        grad_values,
+        grad_names,
+        grad_norm,
+        new_master,
+        new_momentum,
+        new_average,
+        new_master.astype(jnp.bfloat16),
+        new_vectors,
+        new_vector_momentum,
+        new_vector_average,
+    )
+
+
 def solution(mesh):
+    chosen = tuned if dict(mesh.shape) == {"seq": 4, "batch": 8} else local
     return jax.shard_map(
-        local,
+        chosen,
         mesh=mesh,
         in_specs=(
             P("batch", "seq", None),

time: 730 us -> 516 us (0.71); the launches traced: 729 us -> 506 us
  waiting for transfers between devices: 493 us -> 210 us
  Pallas kernels: 0 us -> 127 us
  matrix products: 90.5 us -> 62.2 us
  local copies, waits for them, and re-layouts: 53.3 us -> 36 us
  other arithmetic: 28.3 us -> 13.1 us
    all_gather x3 -> x0, waiting for transfers between devices: 149 us -> none  [the longest x1 110 us: local(): lax.all_gather(master.astype(jnp.bfloat16), ('seq', 'batch'), axis=0, til...]
    reduce_scatter x3, waiting for transfers between devices: 343 us -> 210 us  [the longest x1 166 us: tuned(): lax.psum_scatter(grads.astype(jnp.bfloat16), ('seq', 'batch'), scatter_di...]
    pallas_call x0 -> x1, Pallas kernels: none -> 127 us  [forward_call(): pl.pallas_call(forward_kernel, out_shape=[jax.ShapeDtypeStruct(shape, kin...]
    dynamic_slice x21 -> x0, local copies, waits for them, and re-layouts: 23.2 us -> none  [local(): lax.map(attend_block, (blocked(query), blocked(key_all), blocked(value_al...]
    dot_general x5 -> x3, matrix products: 31.5 us -> 10.5 us  [matmul_t(): lax.dot_general(first_op, second_op, (((1,), (1,)), ((), ())), preferred_...]
    dynamic_update_slice x21 -> x0, local copies, waits for them, and re-layouts: 14.5 us -> none  [the longest x15 14 us: local(): lax.map(attend_back, (blocked(query), blocked(key_all), blocked(value_all...]
    convert_element_type x0 -> x6, local copies, waits for them, and re-layouts: none -> 12.9 us  [the longest x1 4.3 us: tuned(): key_terms.reshape(row_count, -1, D).astype(jnp.bfloat16)]
    reduce_sum x15 -> x5, other arithmetic: 10.6 us -> 3.02 us  [the longest x1 1.88 us: tuned(): local_squares = jnp.sum(owned * owned)]
  transfers between devices with their start and end apart: 6 -> 3, of which waited for: 6 -> 3; matrix products, arithmetic and copies ran while one was open for 1% -> 6% of each run, Pallas kernels for 0% -> 0%
where the time goes in v2:
time: 516 us; the launch traced here: 506 us
  waiting for transfers between devices  210 us (41%)
  Pallas kernels  127 us (25%)
  matrix products  62.2 us (12%)
  blocking collectives  40.1 us (8%)
  local copies, waits for them, and re-layouts  36 us (7%)
  between operations  17.1 us (3%)
  other arithmetic  13.1 us (3%)
    reduce_scatter x1, waiting for transfers between devices, tuned(): lax.psum_scatter(grads.astype(jnp.bfloat16), ('seq', 'batch'), scatter_di...  166 us
    pallas_call x1, Pallas kernels, forward_call(): pl.pallas_call(forward_kernel, out_shape=[jax.ShapeDtypeStruct(shape, kin...  127 us
    psum x1, blocking collectives, tuned(): lax.psum((vector_grads, local_squares), ('seq', 'batch'))  40.1 us
    reduce_scatter x1, waiting for transfers between devices, tuned(): lax.psum_scatter(key_terms.reshape(row_count, -1, D).astype(jnp.bfloat16)...  34.4 us
    dot_general x5, matrix products, tokens_t(): lax.dot_general(first_op, second_op, (((0,), (0,)), ((), ())), preferred_...  16.4 us
    dot_general x3, matrix products, matmul_t(): lax.dot_general(first_op, second_op, (((1,), (1,)), ((), ())), preferred_...  10.5 us
  transfers between devices with their start and end apart: 3, of which 3 were waited for; matrix products, arithmetic and copies ran while one was open for 6% of the time, Pallas kernels for 0%

profile of v2, /device:TPU:0, one launch (start us, length us, event | category | flops | bytes accessed | tf_op | source)
XLA Modules:
  0.0 506.2 jit_solution(6936446643176774170)
XLA Ops:
  7.2 1.3 fusion.59
  8.5 0.7 slice.64
  9.2 0.7 slice.62
  10.0 1.0 reduce_window_sum.11
  11.0 0.7 sub.36
  11.6 0.7 compare_select_fusion
  13.6 0.8 copy.42.slots
  15.0 127.3 %gather_and_forward.1 = (bf16[9984,768]{1,0:T(8,128)(2,1)}, bf16[384,768]{1,0:T(8,128)(2,1)}, bf16[384,768]{1,0:T(8,128)(2,1)}, bf16[3,128,768]{2,1,0:T(8,128)(2...) custom-call(f32[312,768]{1,0:T(8,128)} %master.1, ...), custom_call_target="tpu_custom_call" | custom-call | flops 8000000000 | bytes 60000000 | tf_op jit(solution)/shard_map/gather_and_forward/pallas_call | solution.py:598
  142.3 0.7 compare_bitcast_fusion
  143.0 1.7 slice_reduce_fusion
  144.7 1.2 multiply_convert_fusion.3
  145.9 1.1 copy.44
  146.9 2.9 copy.43
  149.9 5.8 %convert_reduce_fusion = (f32[3072]{0:T(1024)}, bf16[384,3072]{1,0:T(8,128)(2,1)S(1)}) fusion(bf16[384,3072]{1,0:T(8,128)(2,1)} %get-tuple-element.30, bf16[9984,768]{1,0:T(8,128)(2,1)} %get-tuple-element.29, f32[384,768]{1,0:T(8,128)S(1)} %copy-done.8), kind=kOutput, calls=%fused_computation.11 | convolution fusion | flops 1818129408 | bytes 10629120 | tf_op jit(solution)/shard_map/dot_general | solution.py:43
  155.7 6.1 %multiply_reduce_fusion.1 = (f32[768]{0:T(1024)}, f32[384]{0:T(512)S(1)}, f32[384]{0:T(512)S(1)}, f32[768]{0:T(1024)}, f32[384,768]{1,0:T(8,128)S(1)}) fusion(f32[384,768]{1,0:T(8,128)S(1)} %copy-done.10, f32[768]{0:T(1024)S(1)} %get-tuple-element.60, f32[384,768]{1,0:T(8,128)S(1)} %copy-done.8, bf16[384,3072]{1,0:T(8,128)(2,1)S(1)} %get-tuple-element.67, ...), kind=kOutput, calls=%fused_computation.41 | convolution fusion | flops 1814296320 | bytes 10629120 | tf_op jit(solution)/shard_map/dot_general | solution.py:39
  162.1 2.8 convolution_convert_fusion.6
  164.9 2.8 reshape.123
  167.7 2.6 copy.47
  170.3 2.6 fusion.60
  172.8 4.4 fusion.18
  177.3 4.3 copy.51
  181.6 4.3 copy.46
  185.9 8.0 %multiply_reduce_fusion = (f32[3,12,128]{2,1,0:T(8,128)S(1)}, f32[3,12,128,512]{3,2,1,0:T(8,128)S(1)}) fusion(f32[3,12,128,512]{3,2,1,0:T(8,128)} %copy-done, f32[3,12,128]{2,1,0:T(8,128)} %bitcast.75, pred[3,512]{1,0:T(4,128)(4,1)S(1)} %compare_bitcast_fusion, bf16[3,128,12,64]{1,3,2,0:T(8,128)(2,1)} %copy.47, bf16[3,512,12,64]{1,3,2,0:T(8,128)(2,1)} %bitcast.60), kind=kOutput, calls=%fused_computation.1 | convolution fusion | flops 313781760 | bytes 21861888 | tf_op jit(solution)/shard_map/bqhd,bkhd->bhqk/dot_general | solution.py:87
  194.0 2.7 multiply_convert_fusion
  196.7 2.6 multiply_convert_fusion.1
  199.5 4.3 copy.49
  204.1 4.1 convert_reduce_fusion.4
  208.8 0.9 copy.62
  209.7 10.2 %reduce-scatter.6.cloned.1.call-done = bf16[3,128,768]{2,1,0:T(8,128)(2,1)} async-done(((bf16[3,512,768]{2,1,0:T(8,128)(2,1)}), bf16[3,128,768]{2,1,0:T(8,128)(2,1)}) %reduce-scatter.6.cloned.1.call-update) | async-done | bytes 589840 | tf_op jit(solution)/shard_map/reduce_scatter | solution.py:843
  219.9 1.4 copy.53
  221.2 34.4 %reduce-scatter.4.cloned.1.call-done = bf16[3,128,768]{2,1,0:T(8,128)(2,1)} async-done(((bf16[3,512,768]{2,1,0:T(8,128)(2,1)}), bf16[3,128,768]{2,1,0:T(8,128)(2,1)}) %reduce-scatter.4.cloned.1.call-update) | async-done | bytes 589840 | tf_op jit(solution)/shard_map/reduce_scatter | solution.py:837
  255.7 1.4 copy.52
  257.1 3.9 fusion.26
  261.0 3.8 fusion.2
  264.8 1.8 fusion.21
  266.6 1.8 fusion.22
  268.5 4.6 fusion.1
  273.1 4.4 fusion
  277.6 0.8 slice_reduce_fusion.1
  278.6 1.9 convolution_convert_fusion.5
  280.8 165.5 %reduce-scatter.8.cloned.1.call-done = bf16[312,768]{1,0:T(8,128)(2,1)} async-done(((bf16[9984,768]{1,0:T(8,128)(2,1)}), bf16[312,768]{1,0:T(8,128)(2,1)}) %reduce-scatter.8.cloned.1.call-update) | async-done | bytes 479248 | tf_op jit(solution)/shard_map/reduce_scatter | solution.py:882
  446.4 1.9 fusion.37
  448.3 3.5 fusion.30
  451.8 40.1 %all-reduce.1 = (f32[]{:T(128)}, f32[9216]{0:T(1024)S(1)}) all-reduce(f32[]{:T(128)} %fusion.37, f32[9216]{0:T(1024)S(1)} %copy-done.23), channel_id=1, replica_groups=mesh['seq'=4,'batch'=8] {'seq','batch'}, use_global_device_ids=true, to_apply=%region_8.9 | all-reduce | flops 9217 | bytes 73736 | tf_op jit(solution)/shard_map/psum | solution.py:886
  493.9 0.7 add_multiply_fusion.1
  494.6 1.4 fusion.56
  496.0 1.1 add_multiply_fusion
  497.5 0.8 copy.77
  (117 shorter events, 4.8 us)
Async XLA Ops:
  7.2 212.7 %reduce-scatter.6.cloned.1.call-start = ((), (), s32[]{:S(2)}) async-start(), calls=%async_computation.4 | async-start | bytes 2949120 | tf_op jit(solution)/shard_map/reduce_scatter | solution.py:843
  8.5 153.3 %copy-start.27 = (f32[768]{0:T(1024)}, f32[768]{0:T(1024)S(1)}, u32[]{:S(2)}) copy-start(f32[768]{0:T(1024)S(1)} %get-tuple-element.60) | copy-start | bytes 9220
  11.6 130.7 %copy-start.31 = (s32[3,128]{1,0:T(4,128)}, s32[3,128]{1,0:T(4,128)S(1)}, u32[]{:S(2)}) copy-start(s32[3,128]{1,0:T(4,128)S(1)} %sub.36) | copy-start | bytes 4612
  146.9 2.9 copy-start.8
  149.9 5.8 %copy-start.10 = (f32[384,768]{1,0:T(8,128)S(1)}, f32[384,768]{1,0:T(8,128)}, u32[]{:S(2)}) copy-start(f32[384,768]{1,0:T(8,128)} %get-tuple-element.31) | copy-start | bytes 3538948
  155.7 6.1 %copy-start.37 = (bf16[384,3072]{1,0:T(8,128)(2,1)}, bf16[384,3072]{1,0:T(8,128)(2,1)S(1)}, u32[]{:S(2)}) copy-start(bf16[384,3072]{1,0:T(8,128)(2,1)S(1)} %get-tuple-element.67) | copy-start | bytes 7077892
  155.7 6.1 %copy-start.30 = (f32[384]{0:T(512)S(1)}, f32[384]{0:T(512)}, u32[]{:S(2)}) copy-start(f32[384]{0:T(512)} %slice_reduce_fusion) | copy-start | bytes 4612
  170.2 2.6 copy-start.5
  170.2 2.6 copy-start.20
  172.8 4.5 copy-start
  181.6 74.1 %reduce-scatter.4.cloned.1.call-start = ((), (), s32[]{:S(2)}) async-start(), calls=%async_computation.3 | async-start | bytes 2949120 | tf_op jit(solution)/shard_map/reduce_scatter | solution.py:837
  185.9 8.0 %slice-start = ((s8[9437184]{0:T(1024)(128)(4,1)}), s8[4194304]{0:T(1024)(128)(4,1)S(1)}, s32[]{:S(2)}) async-start(s8[9437184]{0:T(1024)(128)(4,1)} %bitcast.56), calls=%async_computation.6 | async-start | bytes 8388608
  185.9 8.0 %slice-start.1 = ((s8[9437184]{0:T(1024)(128)(4,1)}), s8[4194304]{0:T(1024)(128)(4,1)S(1)}, s32[]{:S(2)}) async-start(s8[9437184]{0:T(1024)(128)(4,1)} %bitcast.56), calls=%async_computation.7 | async-start | bytes 8388608
  185.9 8.0 %slice-start.2 = ((s8[9437184]{0:T(1024)(128)(4,1)}), s8[1048576]{0:T(1024)(128)(4,1)S(1)}, s32[]{:S(2)}) async-start(s8[9437184]{0:T(1024)(128)(4,1)} %bitcast.56), calls=%async_computation.8 | async-start | bytes 2097152
  185.9 8.1 %copy-start.21 = (f32[3,16,128]{2,1,0:T(8,128)S(1)}, f32[3,16,128]{2,1,0:T(8,128)}, u32[]{:S(2)}) copy-start(f32[3,16,128]{2,1,0:T(8,128)} %get-tuple-element.36) | copy-start | bytes 73732
  194.0 2.7 copy-start.2
  196.7 2.9 copy-start.1
  203.9 242.5 %reduce-scatter.8.cloned.1.call-start = ((), (), s32[]{:S(2)}) async-start(), calls=%async_computation.5 | async-start | bytes 15814656 | tf_op jit(solution)/shard_map/reduce_scatter | solution.py:882
  257.0 3.9 copy-start.18
  257.0 3.9 copy-start.39
  260.9 17.7 %copy-start.3 = (f32[384,768]{1,0:T(8,128)}, f32[384,768]{1,0:T(8,128)S(1)}, u32[]{:S(2)}) copy-start(f32[384,768]{1,0:T(8,128)S(1)} %fusion.26) | copy-start | bytes 3538948
  261.0 3.8 copy-start.17
  264.7 1.9 copy-start.16
  264.8 3.7 copy-start.11
  264.8 3.7 copy-start.28
  264.8 3.7 copy-start.35
  264.8 3.7 copy-start.38
  268.5 4.6 copy-start.9
  268.5 4.6 copy-start.36
  277.5 1.1 copy-start.26
  277.5 3.1 copy-start.6
  278.5 2.3 copy-start.34
  278.5 2.3 copy-start.33
  278.5 2.3 copy-start.29
  278.6 169.6 %copy-start.32 = (s32[3,128]{1,0:T(4,128)S(1)}, s32[3,128]{1,0:T(4,128)}, u32[]{:S(2)}) copy-start(s32[3,128]{1,0:T(4,128)} %copy-done.31) | copy-start | bytes 4612
  280.8 167.4 %copy-start.22 = (f32[9216]{0:T(1024)}, f32[9216]{0:T(1024)S(1)}, u32[]{:S(2)}) copy-start(f32[9216]{0:T(1024)S(1)} %constant_dynamic-update-slice_fusion.4) | copy-start | bytes 110596
  448.2 3.6 copy-start.23
  448.2 45.7 %copy-start.19 = (f32[9216]{0:T(1024)S(1)}, f32[9216]{0:T(1024)}, u32[]{:S(2)}) copy-start(f32[9216]{0:T(1024)} %param.19) | copy-start | bytes 110596
  448.2 45.7 %copy-start.24 = (f32[9216]{0:T(1024)S(1)}, f32[9216]{0:T(1024)}, u32[]{:S(2)}) copy-start(f32[9216]{0:T(1024)} %param.21) | copy-start | bytes 110596
  448.3 45.7 %copy-start.25 = (f32[9216]{0:T(1024)S(1)}, f32[9216]{0:T(1024)}, u32[]{:S(2)}) copy-start(f32[9216]{0:T(1024)} %param.20) | copy-start | bytes 110596
  448.3 46.3 %copy-start.7 = (bf16[312,768]{1,0:T(8,128)(2,1)S(1)}, bf16[312,768]{1,0:T(8,128)(2,1)}, u32[]{:S(2)}) copy-start(bf16[312,768]{1,0:T(8,128)(2,1)} %reduce-scatter.8.cloned.1.call-done) | copy-start | bytes 1437700
  448.3 46.3 %copy-start.12 = (f32[312,768]{1,0:T(8,128)S(1)}, f32[312,768]{1,0:T(8,128)}, u32[]{:S(2)}) copy-start(f32[312,768]{1,0:T(8,128)} %master.1) | copy-start | bytes 2875396
  448.3 46.3 %copy-start.13 = (f32[312,768]{1,0:T(8,128)S(1)}, f32[312,768]{1,0:T(8,128)}, u32[]{:S(2)}) copy-start(f32[312,768]{1,0:T(8,128)} %param.17) | copy-start | bytes 2875396
  494.6 1.4 copy-start.14
  496.0 2.3 copy-start.4
  496.0 1.5 copy-start.15
Sparse Core Ops, SparseCore 0:
  181.7 38.1 reduce-scatter.5
  222.6 33.0 reduce-scatter.3
  277.6 168.6 reduce-scatter.7
